TPU v7x, 128 devices: a whole 4x4x4 slice. The times are simulated.
128 devices in a mesh: theta: 16 (over z, x), phi: 8 (over y, core).
Axes of the slice: x: 4, y: 4, z: 4, core: 2. Of those that a mesh axis runs over, the one named last changes fastest.
Arguments:
- alm: bfloat16 [512, 2, 8192], P(('theta', 'phi')), may hold values from -6 to 6
- wig: bfloat16 [512, 256, 8192], P(('theta', 'phi')), may hold values from -0.0625 to 0.0625
- slot_order: int32 [512], replicated, may hold values from 0 to 511, each once
- beam: bfloat16 [8192, 128], replicated, may hold values from -6 to 6
- phi_cell: int32 [524288], P(('theta', 'phi')), may hold values from 0 to 192
- theta_cell: int32 [524288], P(('theta', 'phi')), may hold values from 0 to 16
- orient_cell_index: int32 [524288], P(('theta', 'phi')), may hold values from 0 to 127
- tap_weight: float32 [8, 524288], P(None, ('theta', 'phi')), may hold values from 0 to 1
- sample_count: int32 [128], P(('theta', 'phi')), may hold values from 1638 to 4096, as said below
Outputs:
- samples_out: float32 [524288], P(('theta', 'phi'))
Inputs may be any that keep to these rules, and one draw needn't show every extreme that they name: `sample_count`: entry g counts the live samples of device g, which are its first slots; some device has exactly 4096.
All inputs are finite; a program needn't handle non-finite values.
Results may differ from a plain program's by a relative error of at most 0.0062.
Values may be sent and summed in bfloat16 or wider, within the bound.
A program may use at most 192 MiB of HBM per device.

v0:
```python
import math

import jax
import jax.numpy as jnp
from jax import lax
from jax.sharding import PartitionSpec as P

PSI = 128
PD = 192


def padded_2(block, sides, width, periodic):
    for axis, dim in sides:
        count = lax.axis_size(axis)
        forward = [(i, i + 1) for i in range(count - 1)]
        if periodic:
            forward.append((count - 1, 0))
        backward = [(target, source) for source, target in forward]
        low = lax.ppermute(
            lax.slice_in_dim(block, block.shape[dim] - width, None, axis=dim), axis, forward
        )
        high = lax.ppermute(lax.slice_in_dim(block, 0, width, axis=dim), axis, backward)
        block = jnp.concatenate([low, block, high], axis=dim)
    return block


def slot_m_values(slot_order, half_phi, m_all):
    stride = max(half_phi // m_all, 1)
    return slot_order * half_phi // m_all + 7 * slot_order % stride


def weighted_sky(alm_rows, beam, m_value):
    degree = jnp.arange(alm_rows.shape[1], dtype=jnp.int32)
    sky = jnp.where(degree[None, :] >= m_value, alm_rows.astype(jnp.float32), jnp.float32(0.0))
    factor_product = sky[:, :, None] * beam.astype(jnp.float32)[None, :, :]
    return factor_product.astype(jnp.bfloat16)


def cycle_orders(alm_rows, wigner_rows, beam, m_value):
    left_factor = weighted_sky(alm_rows, beam, m_value)
    final_output = jnp.einsum(
        "sh,pht->spt", wigner_rows, left_factor, preferred_element_type=jnp.float32
    )
    return final_output.reshape(final_output.shape[0], -1).astype(jnp.bfloat16)


def phi_table(m_values, phi_index, total_phi, count_m):
    phase = m_values[:, None] * phi_index[None, :] % total_phi
    angle = phase.astype(jnp.float32) * (2.0 * math.pi / total_phi)
    scale = 1.0 / math.sqrt(count_m)
    cosine = jnp.cos(angle) * scale
    sine = jnp.sin(angle) * scale
    table = jnp.stack([jnp.stack([cosine, sine], -1), jnp.stack([-sine, cosine], -1)], 1)
    return table.astype(jnp.bfloat16)


def psi_table(order_count, psi_count):
    orders = jnp.arange(order_count, dtype=jnp.int32)
    points = jnp.arange(psi_count, dtype=jnp.int32)
    phase = orders[:, None] * points[None, :] % psi_count
    angle = phase.astype(jnp.float32) * (2.0 * math.pi / psi_count)
    scale = 1.0 / math.sqrt(2 * order_count)
    return jnp.stack([jnp.cos(angle) * scale, -jnp.sin(angle) * scale], 0).astype(jnp.bfloat16)


def phi_terms(rows, m_values, phi_index, total_phi, count_m):
    table = phi_table(m_values, phi_index, total_phi, count_m)
    data = rows.reshape(rows.shape[0], rows.shape[1], 2, rows.shape[2] // 2)
    return jnp.einsum("ncqd,ntck->qtdk", table, data, preferred_element_type=jnp.float32)


def interpolate(padded, phi_base, theta_base, orient_cell_index, tap_weight, width, psi_count):
    table_rows = padded.reshape(-1, psi_count)
    lane = jnp.arange(psi_count, dtype=jnp.int32)[None, :]
    first_pick = lane == orient_cell_index[:, None]
    second_pick = lane == ((orient_cell_index + 1) % psi_count)[:, None]
    total = jnp.zeros(phi_base.shape, jnp.float32)
    for tap_phi in range(2):
        for tap_theta in range(2):
            place = (phi_base + tap_phi) * width + theta_base + tap_theta
            picked = jnp.take(table_rows, place, axis=0)
            tap_base = 4 * tap_phi + 2 * tap_theta
            weights = jnp.where(first_pick, tap_weight[tap_base][:, None], jnp.float32(0.0))
            weights = weights + jnp.where(
                second_pick, tap_weight[tap_base + 1][:, None], jnp.float32(0.0)
            )
            total = total + jnp.sum(picked * weights, axis=1)
    return total


def shards(
    alm, wig, slot_order, beam, phi_cell, theta_cell, orient_cell_index, tap_weight, sample_count
):
    n_theta = lax.axis_size("theta")
    n_phi = lax.axis_size("phi")
    me_theta = lax.axis_index("theta")
    me_phi = lax.axis_index("phi")
    slots_dev = alm.shape[0]
    m_all = slot_order.shape[0]
    order_count = beam.shape[1]
    cycle_count = wig.shape[1] // n_theta
    total_phi = PD * n_phi
    m_values = slot_m_values(slot_order, total_phi // 2, m_all)
    flat_index = me_theta * n_phi + me_phi
    own_m = lax.dynamic_slice_in_dim(m_values, flat_index * slots_dev, slots_dev)
    orders = jax.vmap(cycle_orders, in_axes=(0, 0, None, 0))(alm, wig, beam, own_m)
    phi_index = me_phi * PD + jnp.arange(PD, dtype=jnp.int32)
    grouped = orders.reshape(slots_dev, n_theta, 1, cycle_count, 2 * order_count)
    grouped = jnp.broadcast_to(grouped, (slots_dev, n_theta, n_phi, cycle_count, 2 * order_count))
    grouped = grouped.reshape(slots_dev, n_theta * n_phi * cycle_count, 2 * order_count)
    received = lax.all_to_all(grouped, ("theta", "phi"), split_axis=1, concat_axis=0, tiled=True)
    spectrum = phi_terms(received, m_values, phi_index, total_phi, m_all)
    spectrum = spectrum.astype(jnp.bfloat16)
    cube = jnp.einsum(
        "qtdk,dkp->qtp", spectrum, psi_table(order_count, PSI), preferred_element_type=jnp.float32
    )
    extended = padded_2(cube, (("phi", 0),), 1, True)
    padded = padded_2(extended, (("theta", 1),), 1, False)
    value = interpolate(
        padded, phi_cell, theta_cell, orient_cell_index, tap_weight, cycle_count + 2, PSI
    )
    live = jnp.arange(phi_cell.shape[0], dtype=jnp.int32) < sample_count[0]
    return jnp.where(live, value, jnp.float32(0.0))


def solution(mesh):
    return jax.shard_map(
        shards,
        mesh=mesh,
        in_specs=(
            P(("theta", "phi"), None, None),
            P(("theta", "phi"), None, None),
            P(),
            P(),
            P(("theta", "phi")),
            P(("theta", "phi")),
            P(("theta", "phi")),
            P(None, ("theta", "phi")),
            P(("theta", "phi")),
        ),
        out_specs=P(("theta", "phi")),
        check_vma=False,
    )
```

profile of v0, /device:TPU:6, one launch (start us, length us, event | category | flops | bytes accessed | tf_op | source)
XLA Modules:
  0.0 191.6 jit_solution(12667190862760332174)
XLA Ops:
  0.0 0.7 add_select_fusion.4
  0.7 0.1 dynamic_slice.3
  0.8 0.1 iota_compare_fusion.2
  0.9 0.0 copy-start
  0.9 4.4 %copy.20 = f32[8192,128]{0,1:T(8,128)} copy(bf16[8192,128]{1,0:T(8,128)(2,1)} %param.14) | data formatting | bytes 6291456 | tf_op jit(solution)/shard_map/vmap()/convert_element_type | solution.py:35
  5.2 0.0 copy-done
  5.2 0.2 convert_select_fusion
  5.4 9.5 %fusion.23 = bf16[4,256,2,128]{1,3,2,0:T(8,128)(2,1)S(1)} fusion(bf16[4,256,8192]{2,1,0:T(8,128)(2,1)} %param.12, f32[8192,128]{0,1:T(8,128)} %copy.20, f32[4,2,8192]{2,1,0:T(2,128)S(1)} %convert_select_fusion), kind=kOutput, calls=%fused_computation.28 | convolution fusion | flops 4312006656 | bytes 21757952 | tf_op jit(solution)/shard_map/vmap(sh,pht->spt)/dot_general | solution.py:41
  14.9 0.5 copy.32
  15.4 0.3 reshape.351
  15.7 4.1 %broadcast_in_dim.113 = bf16[4,16,8,16,256]{4,0,3,2,1:T(4,128)(2,1)} broadcast(bf16[4,16,16,256]{3,0,2,1:T(4,128)(2,1)S(1)} %reshape.351), dimensions={0,1,3,4} | broadcast | bytes 4718592 | tf_op jit(solution)/shard_map/broadcast_in_dim | solution.py:109
  19.8 0.0 copy-start.3
  19.8 0.0 copy-start.4
  19.8 10.9 %all-to-all-start = ((bf16[4,2048,256]{2,0,1:T(4,128)(2,1)}), bf16[4,2048,256]{2,0,1:T(4,128)(2,1)}, u32[]{:S(2)}, u32[]{:S(2)}) async-start(bf16[4,2048,256]{2,0,1:T(4,128)(2,1)} %bitcast.52), calls=%async_computation | async-start | bytes 8388608 | tf_op jit(solution)/shard_map/all_to_all | solution.py:111
  30.8 0.0 copy-start.1
  30.8 0.3 multiply_convert_fusion.7
  31.1 1.9 %fusion.33 = (bf16[512,192,1]{0,1,2:T(8,128)(2,1)S(1)}, bf16[512,192,1]{0,1,2:T(8,128)(2,1)S(1)}, bf16[512,192,1]{0,1,2:T(8,128)(2,1)S(1)}) fusion(s32[192]{0:T(256)S(1)} %iota_add_fusion, s32[512]{0:T(512)S(1)} %add_select_fusion.4), kind=kLoop, calls=%fused_computation.44 | loop fusion | flops 1474560 | bytes 592640 | tf_op jit(solution)/shard_map/convert.9
  33.0 0.1 maximum_bitcast_fusion.2
  33.1 0.0 copy-done.3
  33.1 0.0 copy-done.4
  33.2 0.0 copy-done.1
  33.2 0.1 fusion.52
  33.3 49.1 %all-to-all-done = bf16[4,2048,256]{2,0,1:T(4,128)(2,1)} async-done(((bf16[4,2048,256]{2,0,1:T(4,128)(2,1)}), bf16[4,2048,256]{2,0,1:T(4,128)(2,1)}, u32[]{:S(2)}, u32[]{:S(2)}) %all-to-all-start) | async-done | bytes 4194336 | tf_op jit(solution)/shard_map/all_to_all | solution.py:111
  82.4 2.7 %copy.23 = bf16[4,2048,256]{2,1,0:T(8,128)(2,1)S(1)} copy(bf16[4,2048,256]{2,0,1:T(4,128)(2,1)} %all-to-all-done) | data formatting | bytes 8388608 | tf_op jit(solution)/shard_map/all_to_all | solution.py:111
  85.1 2.6 %copy.24 = bf16[128,4,16,256]{3,2,1,0:T(8,128)(2,1)} copy(bf16[128,4,16,256]{3,2,0,1:T(8,128)(2,1)S(1)} %bitcast.53) | data formatting | bytes 8388608 | tf_op jit(solution)/shard_map/all_to_all | solution.py:111
  87.7 7.0 %reshape.299 = bf16[512,16,2,128]{3,2,1,0:T(2,128)(2,1)} reshape(bf16[128,4,16,256]{3,2,1,0:T(8,128)(2,1)} %copy.24) | data formatting | bytes 8388608 | tf_op jit(solution)/shard_map/reshape | solution.py:68
  94.7 5.3 %fusion.17 = bf16[192,16,2,128]{3,0,2,1:T(8,128)(2,1)S(1)} fusion(bf16[512,16,2,128,1]{3,2,1,0,4:T(2,128)(2,1)} %bitcast.54, bf16[512,1,192,2]{0,2,1,3:T(8,128)(2,1)S(1)} %get-tuple-element.19, bf16[512,1,192,2]{0,2,1,3:T(8,128)(2,1)S(1)} %get-tuple-element.18), kind=kOutput, calls=%fused_computation.26 | convolution fusion | flops 1612972032 | bytes 6553600 | tf_op jit(solution)/shard_map/ncqd,ntck->qtdk/dot_general | solution.py:69
  100.0 0.0 copy-start.2
  100.0 1.0 fusion.14
  101.0 0.0 collective-permute-start
  101.0 2.9 %collective-permute-start.1 = (f32[1,16,128]{2,1,0:T(8,128)S(1)}, f32[1,16,128]{2,1,0:T(8,128)S(1)}, u32[]{:S(2)}, u32[]{:S(2)}) collective-permute-start(f32[1,16,128]{2,1,0:T(8,128)S(1)} %get-tuple-element.17), channel_id=1, source_target_pairs={{1,0},{2,1},{3,2},{4,3},{5,4},{6,5},{7,6},{0,7},{9,8},{10,9},{11,1... | collective-permute-start | bytes 24584 | tf_op jit(solution)/shard_map/ppermute | solution.py:22
  104.0 1.3 collective-permute-done
  105.3 0.0 collective-permute-done.1
  105.4 0.1 pad_maximum_fusion.3
  105.5 3.9 %collective-permute-start.2 = (f32[194,1,128]{2,1,0:T(1,128)S(1)}, f32[194,1,128]{2,1,0:T(1,128)S(1)}, u32[]{:S(2)}, u32[]{:S(2)}) collective-permute-start(f32[194,1,128]{2,1,0:T(1,128)S(1)} %get-tuple-element.14), channel_id=1, source_target_pairs={{0,8},{8,16},{16,24},{24,32},{32,40},{40,48},{48,56},{56,64},{64,7... | collective-permute-start | bytes 297992 | tf_op jit(solution)/shard_map/ppermute | solution.py:19
  109.4 1.9 %collective-permute-start.3 = (f32[194,1,128]{2,1,0:T(1,128)S(1)}, f32[194,1,128]{2,1,0:T(1,128)S(1)}, u32[]{:S(2)}, u32[]{:S(2)}) collective-permute-start(f32[194,1,128]{2,1,0:T(1,128)S(1)} %get-tuple-element.15), channel_id=1, source_target_pairs={{8,0},{16,8},{24,16},{32,24},{40,32},{48,40},{56,48},{64,56},{72,6... | collective-permute-start | bytes 297992 | tf_op jit(solution)/shard_map/ppermute | solution.py:22
  111.4 0.0 copy-done.2
  112.0 0.0 collective-permute-done.2
  112.0 6.0 %collective-permute-done.3 = f32[194,1,128]{2,1,0:T(1,128)S(1)} collective-permute-done((f32[194,1,128]{2,1,0:T(1,128)S(1)}, f32[194,1,128]{2,1,0:T(1,128)S(1)}, u32[]{:S(2)}, u32[]{:S(2)}) %collective-permute-start.3) | collective-permute-done | bytes 99360 | tf_op jit(solution)/shard_map/ppermute | solution.py:22
  118.1 1.8 pad_maximum_fusion
  119.8 1.7 reshape.300
  121.6 14.1 %gather_fusion = f32[4096,128]{1,0:T(8,128)} fusion(f32[3492,128]{1,0:T(8,128)S(1)} %reshape.300, s32[4096]{0:T(1024)S(1)} %get-tuple-element.30), kind=kCustom, calls=%fused_computation.clone | custom fusion | bytes 4210688 | tf_op jit(solution)/shard_map/jit(_take)/gather | solution.py:81
  135.7 14.1 %gather_fusion.2 = f32[4096,128]{1,0:T(8,128)} fusion(f32[3492,128]{1,0:T(8,128)S(1)} %reshape.300, s32[4096]{0:T(1024)S(1)} %get-tuple-element.42), kind=kCustom, calls=%fused_computation.2.clone | custom fusion | bytes 4210688 | tf_op jit(solution)/shard_map/jit(_take)/gather | solution.py:81
  149.8 14.1 %gather_fusion.3 = f32[4096,128]{1,0:T(8,128)} fusion(f32[3492,128]{1,0:T(8,128)S(1)} %reshape.300, s32[4096]{0:T(1024)S(1)} %get-tuple-element.41), kind=kCustom, calls=%fused_computation.3.clone | custom fusion | bytes 4210688 | tf_op jit(solution)/shard_map/jit(_take)/gather | solution.py:81
  163.9 14.1 %gather_fusion.1 = f32[4096,128]{1,0:T(8,128)} fusion(f32[3492,128]{1,0:T(8,128)S(1)} %reshape.300, s32[4096]{0:T(1024)S(1)} %get-tuple-element.31), kind=kCustom, calls=%fused_computation.1.clone | custom fusion | bytes 4210688 | tf_op jit(solution)/shard_map/jit(_take)/gather | solution.py:81
  178.0 13.0 %fusion.8 = (f32[4096]{0:T(1024)S(1)}, f32[4096]{0:T(1024)S(1)}, f32[4096]{0:T(1024)S(1)}, f32[4096]{0:T(1024)S(1)}) fusion(f32[4096,128]{1,0:T(8,128)} %gather_fusion.1, f32[4096]{0:T(1024)S(1)} %bitcast.58, f32[4096]{0:T(1024)S(1)} %bitcast.59, s32[4096]{0:T(1024)S(1)} %add_select_fusion.2, s32[4096]{0:T(1024)S(1)} %copy-done.2, ...), kind=kLoop, calls=%fused_computation.18 | loop fusion | flops 13615104 | bytes 8634368 | tf_op jit(solution)/shard_map/reduce_sum | solution.py:87
  191.0 0.6 add_select_fusion.3
  (6 shorter events, 0.1 us)
Async XLA Ops:
  0.9 4.4 %copy-start = (bf16[4,2,8192]{2,1,0:T(2,128)(2,1)S(1)}, bf16[4,2,8192]{2,1,0:T(2,128)(2,1)}, u32[]{:S(2)}) copy-start(bf16[4,2,8192]{2,1,0:T(2,128)(2,1)} %param.11) | copy-start | bytes 393220
  19.8 13.3 %copy-start.3 = (s32[4096]{0:T(1024)S(1)}, s32[4096]{0:T(1024)}, u32[]{:S(2)}) copy-start(s32[4096]{0:T(1024)} %param.16) | copy-start | bytes 49156
  19.8 13.3 %copy-start.4 = (s32[4096]{0:T(1024)S(1)}, s32[4096]{0:T(1024)}, u32[]{:S(2)}) copy-start(s32[4096]{0:T(1024)} %param.15) | copy-start | bytes 49156
  19.8 62.5 %all-to-all-start = ((bf16[4,2048,256]{2,0,1:T(4,128)(2,1)}), bf16[4,2048,256]{2,0,1:T(4,128)(2,1)}, u32[]{:S(2)}, u32[]{:S(2)}) async-start(bf16[4,2048,256]{2,0,1:T(4,128)(2,1)} %bitcast.52), calls=%async_computation | async-start | bytes 8388608 | tf_op jit(solution)/shard_map/all_to_all | solution.py:111
  30.8 2.4 %copy-start.1 = (f32[8,4096]{1,0:T(8,128)S(1)}, f32[8,4096]{1,0:T(8,128)}, u32[]{:S(2)}) copy-start(f32[8,4096]{1,0:T(8,128)} %param.18) | copy-start | bytes 393220
  100.0 11.4 %copy-start.2 = (s32[4096]{0:T(1024)S(1)}, s32[4096]{0:T(1024)}, u32[]{:S(2)}) copy-start(s32[4096]{0:T(1024)} %param.17) | copy-start | bytes 49156
  101.0 4.3 %collective-permute-start = (f32[1,16,128]{2,1,0:T(8,128)S(1)}, f32[1,16,128]{2,1,0:T(8,128)S(1)}, u32[]{:S(2)}, u32[]{:S(2)}) collective-permute-start(f32[1,16,128]{2,1,0:T(8,128)S(1)} %get-tuple-element.16), channel_id=1, source_target_pairs={{0,1},{1,2},{2,3},{3,4},{4,5},{5,6},{6,7},{7,0},{8,9},{9,10},{10,1... | collective-permute-start | bytes 24584 | tf_op jit(solution)/shard_map/ppermute | solution.py:19
  101.0 4.3 %collective-permute-start.1 = (f32[1,16,128]{2,1,0:T(8,128)S(1)}, f32[1,16,128]{2,1,0:T(8,128)S(1)}, u32[]{:S(2)}, u32[]{:S(2)}) collective-permute-start(f32[1,16,128]{2,1,0:T(8,128)S(1)} %get-tuple-element.17), channel_id=1, source_target_pairs={{1,0},{2,1},{3,2},{4,3},{5,4},{6,5},{7,6},{0,7},{9,8},{10,9},{11,1... | collective-permute-start | bytes 24584 | tf_op jit(solution)/shard_map/ppermute | solution.py:22
  105.5 6.5 %collective-permute-start.2 = (f32[194,1,128]{2,1,0:T(1,128)S(1)}, f32[194,1,128]{2,1,0:T(1,128)S(1)}, u32[]{:S(2)}, u32[]{:S(2)}) collective-permute-start(f32[194,1,128]{2,1,0:T(1,128)S(1)} %get-tuple-element.14), channel_id=1, source_target_pairs={{0,8},{8,16},{16,24},{24,32},{32,40},{40,48},{48,56},{56,64},{64,7... | collective-permute-start | bytes 297992 | tf_op jit(solution)/shard_map/ppermute | solution.py:19
  109.4 8.6 %collective-permute-start.3 = (f32[194,1,128]{2,1,0:T(1,128)S(1)}, f32[194,1,128]{2,1,0:T(1,128)S(1)}, u32[]{:S(2)}, u32[]{:S(2)}) collective-permute-start(f32[194,1,128]{2,1,0:T(1,128)S(1)} %get-tuple-element.15), channel_id=1, source_target_pairs={{8,0},{16,8},{24,16},{32,24},{40,32},{48,40},{56,48},{64,56},{72,6... | collective-permute-start | bytes 297992 | tf_op jit(solution)/shard_map/ppermute | solution.py:22
where the time goes:
time: 192 us
  local copies, waits for them, and re-layouts  79.9 us (42%)
  waiting for transfers between devices  56.4 us (29%)
  starting transfers between devices  19.8 us (10%)
  other arithmetic  18.9 us (10%)
  matrix products  15.8 us (8%)
    gather x4, local copies, waits for them, and re-layouts, interpolate(): picked = jnp.take(table_rows, place, axis=0)  56.4 us
    all_to_all x1, waiting for transfers between devices, shards(): lax.all_to_all(grouped, ('theta', 'phi'), split_axis=1, concat_axis=0, ti...  49.1 us
    reduce_sum x1, other arithmetic, interpolate(): total = total + jnp.sum(picked * weights, axis=1)  13 us
    all_to_all x1, starting transfers between devices, shards(): lax.all_to_all(grouped, ('theta', 'phi'), split_axis=1, concat_axis=0, ti...  10.9 us
    dot_general x1, matrix products, cycle_orders(): jnp.einsum('sh,pht->spt', wigner_rows, left_factor, preferred_element_typ...  9.46 us
    reshape x1, local copies, waits for them, and re-layouts, phi_terms(): data = rows.reshape(rows.shape[0], rows.shape[1], 2, rows.shape[2] // 2)  6.96 us
    ppermute x2, waiting for transfers between devices, padded_2(): lax.ppermute(lax.slice_in_dim(block, 0, width, axis=dim), axis, backward)  6.05 us
    all_to_all x2, local copies, waits for them, and re-layouts, shards(): lax.all_to_all(grouped, ('theta', 'phi'), split_axis=1, concat_axis=0, ti...  5.32 us
  transfers between devices with their start and end apart: 5, of which 3 were waited for; matrix products, arithmetic and copies ran while one was open for 1% of the time, Pallas kernels for 0%

commit v1 on v0

v1 whole, which is shorter than its diff:
```python
import functools
import math

import jax
import jax.numpy as jnp
from jax import lax
from jax.experimental import pallas as pl
from jax.experimental.pallas import tpu as pltpu
from jax.sharding import PartitionSpec as P

PSI = 128
PD = 192
QP = 200
CH = 4
MESH = pl.DeviceIdType.MESH
ORDER = (0, 3, 1, 2)


def slot_m(order, half, m_all):
    stride = max(half // m_all, 1)
    m = lax.shift_right_logical(order * half, m_all.bit_length() - 1)
    if stride > 1:
        m = m + (7 * order) % stride
    return m


def turn_cos(phase, total):
    x = (jnp.abs(phase - total / 2) - total / 4) * (2.0 * math.pi / total)
    x2 = x * x
    p = jnp.float32(-1.0 / math.factorial(11))
    for n in (9, 7, 5, 3, 1):
        p = p * x2 + jnp.float32((-1) ** (n // 2) / math.factorial(n))
    return p * x


def wrap(value, total):
    return value - jnp.floor((value + 0.5) * jnp.float32(1.0 / total)) * total


def orders_kernel(
    n_theta, n_phi, slots, ldeg, tile, m_all,
    wig_hbm, alm_ref, beam_hbm, order_ref, order_smem, cube_ref,
    wig_v, beam_v, beam_t, x32, x16, landed, grid_v, table_v, halo_v,
    wig_sem, beam_sem, a_send, a_recv, y_send, y_recv, f_send, f_recv, s_send, s_recv, h_send, h_recv,
):
    me_t = lax.axis_index("theta")
    me_p = lax.axis_index("phi")
    me_y, me_c = me_p // 2, me_p % 2
    n_y = n_phi // 2
    total = PD * n_phi
    rt = 4 * CH
    rows = rt * 8 // CH
    per = rt // CH
    tiles = ldeg // tile

    def at(t, y, c):
        return (t, y * 2 + c)

    y_up, y_down, y_far = (me_y + 1) % n_y, (me_y + n_y - 1) % n_y, (me_y + 2) % n_y
    own = me_p
    block = {"own": own, "down": y_down * 2 + me_c, "up": y_up * 2 + me_c, "far": y_far * 2 + me_c}

    beam_copy = pltpu.make_async_copy(beam_hbm, beam_v, beam_sem)
    beam_copy.start()

    def wig_copy(s, i):
        span = pl.ds(i * tile, tile)
        return pltpu.make_async_copy(wig_hbm.at[s, :, span], wig_v.at[s, :, span], wig_sem.at[s, i])

    for s in range(slots):
        for i in range(tiles):
            wig_copy(s, i).start()

    barrier = pltpu.get_barrier_semaphore()

    def greet(k, _):
        pl.semaphore_signal(
            barrier, inc=1, device_id=at(lax.rem(me_t + k, n_theta), me_y, me_c), device_id_type=MESH
        )
        return 0

    lax.fori_loop(1, n_theta, greet, 0)
    for y, c in ((y_up, me_c), (y_down, me_c), (me_y, 1 - me_c)):
        pl.semaphore_signal(barrier, inc=1, device_id=at(me_t, y, c), device_id_type=MESH)

    eye = (
        lax.broadcasted_iota(jnp.int32, (128, 128), 0) == lax.broadcasted_iota(jnp.int32, (128, 128), 1)
    ).astype(jnp.bfloat16)
    beam_copy.wait()
    for i in range(tiles):
        beam_t[:, i * tile:(i + 1) * tile] = lax.dot_general(
            eye, beam_v[i * tile:(i + 1) * tile, :], (((1,), (1,)), ((), ())),
            preferred_element_type=jnp.float32,
        ).astype(jnp.bfloat16)

    k_at = lax.broadcasted_iota(jnp.int32, (128, 128), 0)
    p_at = lax.broadcasted_iota(jnp.int32, (128, 128), 1)
    turn = ((k_at * p_at) % PSI).astype(jnp.float32)
    scale = 1.0 / math.sqrt(2 * 128)
    psi0 = (turn_cos(turn, PSI) * scale).astype(jnp.bfloat16)
    psi1 = (-turn_cos(wrap(turn - PSI / 4 + PSI, PSI), PSI) * scale).astype(jnp.bfloat16)
    psi = jnp.concatenate(
        [jnp.concatenate([psi0, psi1], axis=1), jnp.concatenate([psi1, -psi0], axis=1)], axis=0
    )

    for s in range(slots):
        m_own = slot_m(order_smem[(me_t * n_phi + me_p) * slots + s], total // 2, m_all)
        acc = None
        for i in range(tiles):
            degree = lax.broadcasted_iota(jnp.int32, (2, tile), 1) + i * tile
            sky = jnp.where(
                degree >= m_own, alm_ref[s, :, i * tile:(i + 1) * tile].astype(jnp.float32), 0.0
            )
            part = beam_t[:, i * tile:(i + 1) * tile]
            weighted = jnp.concatenate(
                [
                    part * jnp.broadcast_to(sky[c:c + 1, :], (128, tile)).astype(jnp.bfloat16)
                    for c in range(2)
                ],
                axis=0,
            )
            wig_copy(s, i).wait()
            term = lax.dot_general(
                weighted, wig_v[s, :, i * tile:(i + 1) * tile], (((1,), (1,)), ((), ())),
                preferred_element_type=jnp.float32,
            )
            acc = term if acc is None else acc + term
        x = lax.dot_general(
            acc.astype(jnp.bfloat16), psi, (((0,), (0,)), ((), ())), preferred_element_type=jnp.float32
        )
        for c in range(2):
            x32[pl.ds(2 * s + c, n_theta * rt, stride=8), :] = x[:, c * 128:(c + 1) * 128]

    x16[...] = x32[...].astype(jnp.bfloat16)
    pl.semaphore_wait(barrier, n_theta + 2)

    for j in ORDER:
        def send(k, _):
            t = lax.rem(me_t + k, n_theta)
            src = x16.at[pl.ds(pl.multiple_of(t * rt * 8 + j * rows, 16), rows), :]
            pltpu.make_async_remote_copy(
                src_ref=src, dst_ref=landed.at[j, me_t], send_sem=a_send.at[j], recv_sem=a_recv.at[j],
                device_id=at(t, me_y, me_c), device_id_type=MESH,
            ).start()
            return 0

        lax.fori_loop(1, n_theta, send, 0)
        landed[j, me_t] = x16[pl.ds(pl.multiple_of(me_t * rt * 8 + j * rows, 16), rows), :]

    k_all = n_phi * n_theta * 2 * slots
    so = order_ref[...]
    m_row = slot_m(so, total // 2, m_all)
    m_hi = lax.shift_right_logical(m_row, 4).astype(jnp.float32)
    m_lo = (m_row & 15).astype(jnp.float32)
    both = jnp.concatenate([m_hi, m_lo, jnp.zeros((6, m_all), jnp.float32)], axis=0).astype(jnp.bfloat16)
    n_at = lax.broadcasted_iota(jnp.int32, (m_all, k_all), 0)
    col = lax.broadcasted_iota(jnp.int32, (m_all, k_all), 1)
    per_block = n_theta * 2 * slots
    slot_at = (col % per_block // (2 * slots) * n_phi + col // per_block) * slots + col % (2 * slots) // 2
    pick = (n_at == slot_at).astype(jnp.bfloat16)
    moved = jnp.dot(both, pick, preferred_element_type=jnp.float32)
    m_col = moved[0:1, :] * 16.0 + moved[1:2, :]
    q_at = lax.broadcasted_iota(jnp.int32, (QP, k_all), 0) + (me_p * PD - 1 + total)
    part_at = (lax.broadcasted_iota(jnp.int32, (1, k_all), 1) % 2).astype(jnp.float32)
    phase = wrap(m_col * q_at.astype(jnp.float32) + (1.0 - part_at * 0.25) * total, total)
    table_v[...] = (turn_cos(phase, total) * (1.0 / math.sqrt(m_all))).astype(jnp.bfloat16)

    def share(j, which, n):
        b = block[which]
        return pltpu.make_async_remote_copy(
            src_ref=grid_v.at[j, b], dst_ref=grid_v.at[j, b], send_sem=s_send.at[j, n], recv_sem=s_recv.at[j, n],
            device_id=at(me_t, me_y, 1 - me_c), device_id_type=MESH,
        )

    def pass_y(j, n, up):
        return pltpu.make_async_remote_copy(
            src_ref=grid_v.at[j, own], dst_ref=grid_v.at[j, own], send_sem=y_send.at[j, n],
            recv_sem=y_recv.at[j, n], device_id=at(me_t, y_up if up else y_down, me_c), device_id_type=MESH,
        )

    def forward(j, n, up):
        half = pl.ds(n * (per // 2), per // 2)
        b = block["down" if up else "up"]
        return pltpu.make_async_remote_copy(
            src_ref=grid_v.at[j, b, half], dst_ref=grid_v.at[j, b, half], send_sem=f_send.at[j, n],
            recv_sem=f_recv.at[j, n], device_id=at(me_t, y_up if up else y_down, me_c), device_id_type=MESH,
        )

    for j in ORDER:
        pltpu.make_async_remote_copy(
            src_ref=landed.at[j, pl.ds(0, n_theta - 1)], dst_ref=landed.at[j, pl.ds(0, n_theta - 1)],
            send_sem=a_send.at[j], recv_sem=a_recv.at[j], device_id=at(me_t, me_y, me_c), device_id_type=MESH,
        ).wait_recv()
        for pair in range(per // 2):
            both_r = landed[j, :, pair * 16:(pair + 1) * 16, :].astype(jnp.float32)
            for n in range(2):
                grid_v[j, own, 2 * pair + n] = (
                    both_r[:, n * 8:(n + 1) * 8, :].reshape(n_theta * 8, 128).astype(jnp.bfloat16)
                )
        pass_y(j, 0, True).start()
        pass_y(j, 1, False).start()
        share(j, "own", 0).start()

    for j in ORDER:
        pass_y(j, 0, True).wait_recv()
        forward(j, 0, True).start()
        share(j, "down", 1).start()
        pass_y(j, 1, False).wait_recv()
        forward(j, 1, False).start()
        share(j, "up", 2).start()

    def halo(n, row):
        t = me_t + 1 if n == 0 else me_t - 1
        return pltpu.make_async_remote_copy(
            src_ref=cube_ref.at[row], dst_ref=halo_v.at[n], send_sem=h_send.at[n], recv_sem=h_recv.at[n],
            device_id=at(lax.rem(t + n_theta, n_theta), me_y, me_c), device_id_type=MESH,
        )

    for j in ORDER:
        forward(j, 0, True).wait_recv()
        forward(j, 1, False).wait_recv()
        share(j, "far", 3).start()
        for n, which in enumerate(("own", "down", "up", "far")):
            share(j, which, n).wait_recv()
        for pair in range(per // 2):
            right = jnp.concatenate(
                [grid_v[j, :, 2 * pair + n].reshape(k_all, 128) for n in range(2)], axis=1
            )
            tile_out = jnp.dot(table_v[...], right, preferred_element_type=jnp.float32)
            for n in range(2):
                cube_ref[1 + j * per + 2 * pair + n] = tile_out[:, n * 128:(n + 1) * 128]
        if j == CH - 1:
            @pl.when(me_t < n_theta - 1)
            def _():
                halo(0, rt).start()
        if j == 0:
            @pl.when(me_t > 0)
            def _():
                halo(1, 1).start()

    @pl.when(me_t > 0)
    def _():
        halo(0, rt).wait_recv()
        cube_ref[0] = halo_v[0]

    @pl.when(me_t == 0)
    def _():
        cube_ref[0] = jnp.zeros((QP, 128), jnp.float32)

    @pl.when(me_t < n_theta - 1)
    def _():
        halo(1, 1).wait_recv()
        cube_ref[rt + 1] = halo_v[1]
        halo(0, rt).wait_send()

    @pl.when(me_t == n_theta - 1)
    def _():
        cube_ref[rt + 1] = jnp.zeros((QP, 128), jnp.float32)

    @pl.when(me_t > 0)
    def _():
        halo(1, 1).wait_send()

    for j in ORDER:
        pltpu.make_async_remote_copy(
            src_ref=landed.at[j, pl.ds(0, n_theta - 1)], dst_ref=landed.at[j, pl.ds(0, n_theta - 1)],
            send_sem=a_send.at[j], recv_sem=a_recv.at[j], device_id=at(me_t, me_y, me_c), device_id_type=MESH,
        ).wait_send()
        pass_y(j, 0, True).wait_send()
        pass_y(j, 1, False).wait_send()
        forward(j, 0, True).wait_send()
        forward(j, 1, False).wait_send()
        for n, which in enumerate(("own", "down", "up", "far")):
            share(j, which, n).wait_send()


def make_cube(alm, wig, slot_order, beam):
    n_theta, n_phi = lax.axis_size("theta"), lax.axis_size("phi")
    slots, _, ldeg = alm.shape
    m_all = slot_order.shape[0]
    rt = 4 * CH
    per = rt // CH
    tile = min(ldeg, 2048)
    vmem = pl.BlockSpec(memory_space=pltpu.VMEM)
    anywhere = pl.BlockSpec(memory_space=pl.ANY)
    k_all = n_phi * n_theta * 2 * slots
    return pl.pallas_call(
        functools.partial(orders_kernel, n_theta, n_phi, slots, ldeg, tile, m_all),
        out_shape=jax.ShapeDtypeStruct((rt + 2, QP, 128), jnp.float32),
        in_specs=[anywhere, vmem, anywhere, vmem, pl.BlockSpec(memory_space=pltpu.SMEM)],
        out_specs=vmem,
        scratch_shapes=[
            pltpu.VMEM(wig.shape, jnp.bfloat16),
            pltpu.VMEM(beam.shape, jnp.bfloat16),
            pltpu.VMEM(beam.shape[::-1], jnp.bfloat16),
            pltpu.VMEM((n_theta * rt * 8, 128), jnp.float32),
            pltpu.VMEM((n_theta * rt * 8, 128), jnp.bfloat16),
            pltpu.VMEM((CH, n_theta, per * 8, 128), jnp.bfloat16),
            pltpu.VMEM((CH, n_phi, per, n_theta * 8, 128), jnp.bfloat16),
            pltpu.VMEM((QP, k_all), jnp.bfloat16),
            pltpu.VMEM((2, QP, 128), jnp.float32),
            pltpu.SemaphoreType.DMA((slots, ldeg // tile)),
            pltpu.SemaphoreType.DMA,
            pltpu.SemaphoreType.DMA((CH,)),
            pltpu.SemaphoreType.DMA((CH,)),
            pltpu.SemaphoreType.DMA((CH, 2)),
            pltpu.SemaphoreType.DMA((CH, 2)),
            pltpu.SemaphoreType.DMA((CH, 2)),
            pltpu.SemaphoreType.DMA((CH, 2)),
            pltpu.SemaphoreType.DMA((CH, 4)),
            pltpu.SemaphoreType.DMA((CH, 4)),
            pltpu.SemaphoreType.DMA((2,)),
            pltpu.SemaphoreType.DMA((2,)),
        ],
        compiler_params=pltpu.CompilerParams(
            collective_id=0, has_side_effects=True, vmem_limit_bytes=56 << 20
        ),
        name="make_cube",
    )(wig, alm, beam, slot_order.reshape(1, -1), slot_order)


def sample_kernel(cells, base_ref, shift_ref, count_ref, cube_ref, weight_ref, out_ref, taps):
    def build(r, _):
        first = cube_ref[r]
        for e, rows in ((0, first), (1, pltpu.roll(first, PSI - 1, 1))):
            @pl.when(r < cells)
            def _():
                taps[pl.ds(r * QP * 4 + e, QP, stride=4), :] = rows

            @pl.when(r >= 1)
            def _():
                taps[pl.ds((r - 1) * QP * 4 + 2 + e, QP, stride=4), :] = rows

        return 0

    lax.fori_loop(0, cells + 1, build, 0)
    lane = lax.broadcasted_iota(jnp.int32, (8, 128), 1)
    count = count_ref[0]

    def group(g, _):
        picked = jnp.zeros((8, 128), jnp.float32)
        for n in range(128):
            i = g * 128 + n
            rows = taps[pl.ds(pl.multiple_of(base_ref[i], 4), 8), :]
            picked = jnp.where(lane == n, pltpu.roll(rows, shift_ref[i], 1), picked)
        weights = weight_ref[:, pl.ds(pl.multiple_of(g * 128, 128), 128)]
        value = jnp.sum(picked * weights, axis=0, keepdims=True)
        out_ref[pl.ds(g, 1), :] = jnp.where(lane[0:1, :] + g * 128 < count, value, 0.0)
        return 0

    lax.fori_loop(0, out_ref.shape[0], group, 0)


def shards(
    alm, wig, slot_order, beam, phi_cell, theta_cell, orient_cell_index, tap_weight, sample_count
):
    cube = make_cube(alm, wig, slot_order, beam)
    cells = cube.shape[0] - 1
    samples = phi_cell.shape[0]
    base = (theta_cell * QP + phi_cell) * 4
    shift = (jnp.arange(samples, dtype=jnp.int32) - orient_cell_index) & (PSI - 1)
    smem = pl.BlockSpec(memory_space=pltpu.SMEM)
    vmem = pl.BlockSpec(memory_space=pltpu.VMEM)
    value = pl.pallas_call(
        functools.partial(sample_kernel, cells),
        out_shape=jax.ShapeDtypeStruct((samples // 128, 128), jnp.float32),
        in_specs=[smem, smem, smem, vmem, vmem],
        out_specs=vmem,
        scratch_shapes=[pltpu.VMEM((cells * QP * 4 + 8, 128), jnp.float32)],
        compiler_params=pltpu.CompilerParams(vmem_limit_bytes=24 << 20),
        name="take_samples",
    )(base, shift, sample_count, cube, tap_weight)
    return value.reshape(-1)


def solution(mesh):
    return jax.shard_map(
        shards,
        mesh=mesh,
        in_specs=(
            P(("theta", "phi"), None, None),
            P(("theta", "phi"), None, None),
            P(),
            P(),
            P(("theta", "phi")),
            P(("theta", "phi")),
            P(("theta", "phi")),
            P(None, ("theta", "phi")),
            P(("theta", "phi")),
        ),
        out_specs=P(("theta", "phi")),
        check_vma=False,
    )
```

time: 192 us -> 70.3 us (0.37)
  the two profiles are of different devices: /device:TPU:6 before, /device:TPU:1 now
where the time goes in v1:
time: 70.3 us; the launch traced here: 70.1 us
  Pallas kernels  67.1 us (95%)
  local copies, waits for them, and re-layouts  1.5 us (2%)
  other arithmetic  0.76 us (1%)
    pallas_call x1, Pallas kernels, make_cube(): pl.pallas_call(functools.partial(orders_kernel, n_theta, n_phi, slots, ld...  55.3 us
    pallas_call x1, Pallas kernels, shards(): pl.pallas_call(functools.partial(sample_kernel, cells), out_shape=jax.Sha...  11.8 us
    unnamed x4, local copies, waits for them, and re-layouts  1.5 us

profile of v1, /device:TPU:1, one launch (start us, length us, event | category | flops | bytes accessed | tf_op | source)
XLA Modules:
  0.0 70.1 jit_solution(13767180798346920290)
XLA Ops:
  0.7 0.8 %subtract_and_fusion = (s32[4096]{0:T(1024)S(1)}, s32[4096]{0:T(1024)S(1)}) fusion(s32[4096]{0:T(1024)} %param.15, s32[4096]{0:T(1024)} %param.13, s32[4096]{0:T(1024)} %param.14), kind=kLoop, calls=%fused_computation | loop fusion | flops 20480 | bytes 81920 | tf_op jit(solution)/shard_map/and | solution.py:361
  1.4 0.0 copy-start.1
  1.4 55.3 %make_cube.1.cube_ref = f32[18,200,128]{2,1,0:T(8,128)} custom-call(bf16[4,256,8192]{2,1,0:T(8,128)(2,1)} %wig_hbm.1, bf16[4,2,8192]{2,1,0:T(2,128)(2,1)} %alm_ref.1, bf16[8192,128]{1,0:T(8,128)(2,1)} %beam_hbm.1, s32[1,512]{1,0:T(1,128)} %bitcast.2, s32[512]{0:T(512)} %order_smem.1), custom_call_target="tpu_custom_call" | custom-call | tf_op jit(solution)/shard_map/make_cube/pallas_call | solution.py:287
  56.7 0.0 copy-done.1
  56.7 0.0 copy-start
  56.7 1.5 %copy-done = f32[18,200,128]{2,1,0:T(8,128)S(1)} copy-done((f32[18,200,128]{2,1,0:T(8,128)S(1)}, f32[18,200,128]{2,1,0:T(8,128)}, u32[]{:S(2)}) %copy-start) | copy-done | bytes 1843224
  58.2 11.8 %take_samples.1 = f32[32,128]{1,0:T(8,128)} custom-call(s32[4096]{0:T(1024)S(1)} %get-tuple-element.6.base_ref, s32[4096]{0:T(1024)S(1)} %get-tuple-element.5.shift_ref, s32[1]{0:T(128)S(6)} %copy.10.count_ref, f32[18,200,128]{2,1,0:T(8,128)S(1)} %copy-done, f32[8,4096]{1,0:T(8,128)S(1)} %copy-done.1), custom_call_target="tpu_custom_call" | custom-call | tf_op jit(solution)/shard_map/take_samples/pallas_call | solution.py:364
Async XLA Ops:
  1.4 55.3 %copy-start.1 = (f32[8,4096]{1,0:T(8,128)S(1)}, f32[8,4096]{1,0:T(8,128)}, u32[]{:S(2)}) copy-start(f32[8,4096]{1,0:T(8,128)} %weight_ref.1) | copy-start | bytes 393220
  56.7 1.5 %copy-start = (f32[18,200,128]{2,1,0:T(8,128)S(1)}, f32[18,200,128]{2,1,0:T(8,128)}, u32[]{:S(2)}) copy-start(f32[18,200,128]{2,1,0:T(8,128)} %make_cube.1.cube_ref) | copy-start | bytes 5529604

commit v2 on v0

v2 whole, which is shorter than its diff:
```python
import functools
import math

import jax
import jax.numpy as jnp
from jax import lax
from jax.experimental import pallas as pl
from jax.experimental.pallas import tpu as pltpu
from jax.sharding import PartitionSpec as P

PSI = 128
PD = 192
RT = 16
QP = 200
CH = 4
PER = RT // CH
MESH = pl.DeviceIdType.MESH
NT = (((1,), (1,)), ((), ()))
TN = (((0,), (0,)), ((), ()))


def slot_m(order, half, m_all):
    stride = max(half // m_all, 1)
    m = lax.shift_right_logical(order * half, m_all.bit_length() - 1)
    if stride > 1:
        m = m + (7 * order) % stride
    return m


def turn_cos(phase, total):
    x = (jnp.abs(phase - total / 2) - total / 4) * (2.0 * math.pi / total)
    x2 = x * x
    p = jnp.float32(-1.0 / math.factorial(11))
    for n in (9, 7, 5, 3, 1):
        p = p * x2 + jnp.float32((-1) ** (n // 2) / math.factorial(n))
    return p * x


def wrap(value, total):
    return value - jnp.floor((value + 0.5) * jnp.float32(1.0 / total)) * total


def psi_rows():
    k_at = lax.broadcasted_iota(jnp.int32, (128, 128), 0)
    p_at = lax.broadcasted_iota(jnp.int32, (128, 128), 1)
    turn = ((k_at * p_at) & (PSI - 1)).astype(jnp.float32)
    scale = 1.0 / math.sqrt(2 * 128)
    psi0 = turn_cos(turn, PSI) * scale
    psi1 = -turn_cos(wrap(turn + 0.75 * PSI, PSI), PSI) * scale
    return psi0.astype(jnp.bfloat16), psi1.astype(jnp.bfloat16), (-psi0).astype(jnp.bfloat16)


def kernel(
    n_theta, n_phi, slots, ldeg, tile, m_all, groups,
    wig_hbm, alm_hbm, beam_hbm, order_hbm, phi_hbm, theta_hbm, orient_hbm, weight_hbm, out_ref,
    wig_v, beam_v, beam_t, alm_v, order_v, cells_v, weight_v, psi_v, sums, x32, x16, landed, grid_v,
    table_v, halo_out, halo_in, taps, index_v, base_s, orient_s,
    wig_sem, in_sem, idx_sem, a_send, a_recv, y_send, y_recv, f_send, f_recv, s_send, s_recv, h_send, h_recv,
):
    me_t = lax.axis_index("theta")
    me_p = lax.axis_index("phi")
    me_y, me_c = me_p // 2, me_p % 2
    n_y = n_phi // 2
    total = PD * n_phi
    rows = PER * 8
    tiles = ldeg // tile
    k_all = n_phi * n_theta * 2 * slots
    per_block = n_theta * 2 * slots

    y_up, y_down, y_far = (me_y + 1) % n_y, (me_y + n_y - 1) % n_y, (me_y + 2) % n_y
    own = me_p
    block = (own, y_down * 2 + me_c, y_up * 2 + me_c, y_far * 2 + me_c)

    def at(t, y, c):
        return (t, y * 2 + c)

    def chunk(n):
        return (3 * n) % CH

    reads = [
        pltpu.make_async_copy(src, dst, in_sem.at[n])
        for n, (src, dst) in enumerate(
            (
                (beam_hbm, beam_v), (alm_hbm, alm_v), (order_hbm, order_v), (phi_hbm, cells_v.at[0]),
                (theta_hbm, cells_v.at[1]), (orient_hbm, cells_v.at[2]), (weight_hbm, weight_v),
            )
        )
    ]

    def wig_copy(n):
        span = pl.ds(pl.multiple_of(n // slots * tile, 128), tile)
        return pltpu.make_async_copy(wig_hbm.at[n % slots, :, span], wig_v.at[n], wig_sem.at[n])

    for r in reads[:3]:
        r.start()

    def wig_start(n, _):
        wig_copy(n).start()
        return 0

    lax.fori_loop(0, slots * tiles, wig_start, 0)
    for r in reads[3:]:
        r.start()

    barrier = pltpu.get_barrier_semaphore()

    def greet(k, _):
        pl.semaphore_signal(
            barrier, inc=1, device_id=at(lax.rem(me_t + k, n_theta), me_y, me_c), device_id_type=MESH
        )
        return 0

    lax.fori_loop(1, n_theta, greet, 0)
    for y, c in ((y_up, me_c), (y_down, me_c), (me_y, 1 - me_c)):
        pl.semaphore_signal(barrier, inc=1, device_id=at(me_t, y, c), device_id_type=MESH)

    psi0, psi1, psi2 = psi_rows()
    psi_v[:128, :128] = psi0
    psi_v[:128, 128:] = psi1
    psi_v[128:, :128] = psi1
    psi_v[128:, 128:] = psi2
    for r in reads[:3]:
        r.wait()

    order_row = order_v[...]
    m_row = slot_m(order_row, total // 2, m_all)
    slot_lane = lax.broadcasted_iota(jnp.int32, (1, m_all), 1)
    eye = (
        lax.broadcasted_iota(jnp.int32, (128, 128), 0) == lax.broadcasted_iota(jnp.int32, (128, 128), 1)
    ).astype(jnp.bfloat16)

    def stage(n, _):
        i, s = n // slots, n % slots

        @pl.when(s == 0)
        def _():
            beam_t[...] = lax.dot_general(
                eye, beam_v[pl.ds(pl.multiple_of(i * tile, 128), tile), :], NT, preferred_element_type=jnp.float32
            ).astype(jnp.bfloat16)

        mine = slot_lane == (me_t * n_phi + me_p) * slots + s
        m_own = jnp.sum(jnp.where(mine, m_row, 0).astype(jnp.float32), axis=1, keepdims=True)
        degree = (lax.broadcasted_iota(jnp.int32, (2, tile), 1) + i * tile).astype(jnp.float32)
        sky = alm_v[s, :, pl.ds(pl.multiple_of(i * tile, 128), tile)].astype(jnp.float32)
        sky = jnp.where(degree >= m_own, sky, 0.0)
        weighted = jnp.concatenate(
            [
                beam_t[...] * jnp.broadcast_to(sky[c:c + 1, :], (128, tile)).astype(jnp.bfloat16)
                for c in range(2)
            ],
            axis=0,
        )
        wig_copy(n).wait()
        term = lax.dot_general(weighted, wig_v[n], NT, preferred_element_type=jnp.float32)

        @pl.when(i == 0)
        def _():
            sums[s] = term

        @pl.when(i > 0)
        def _():
            sums[s] += term

        return 0

    lax.fori_loop(0, slots * tiles, stage, 0)

    def to_psi(s, _):
        x = lax.dot_general(sums[s].astype(jnp.bfloat16), psi_v[...], TN, preferred_element_type=jnp.float32)
        for c in range(2):
            x32[pl.ds(2 * s + c, n_theta * RT, stride=8), :] = x[:, c * 128:(c + 1) * 128]
        return 0

    lax.fori_loop(0, slots, to_psi, 0)

    def narrow(n, _):
        span = pl.ds(pl.multiple_of(n * RT * 8, 16), RT * 8)
        x16[span, :] = x32[span, :].astype(jnp.bfloat16)
        return 0

    lax.fori_loop(0, n_theta, narrow, 0)
    pl.semaphore_wait(barrier, n_theta + 2)

    def x_rows(t, j):
        return pl.ds(pl.multiple_of(t * RT * 8 + j * rows, 16), rows)

    def send(n, _):
        j, k = chunk(n // (n_theta - 1)), n % (n_theta - 1) + 1
        t = lax.rem(me_t + k, n_theta)
        pltpu.make_async_remote_copy(
            src_ref=x16.at[x_rows(t, j), :], dst_ref=landed.at[j, me_t], send_sem=a_send.at[j],
            recv_sem=a_recv.at[j], device_id=at(t, me_y, me_c), device_id_type=MESH,
        ).start()
        return 0

    lax.fori_loop(0, CH * (n_theta - 1), send, 0)

    def landed_all(j):
        others = landed.at[j, pl.ds(0, n_theta - 1)]
        return pltpu.make_async_remote_copy(
            src_ref=others, dst_ref=others, send_sem=a_send.at[j], recv_sem=a_recv.at[j],
            device_id=at(me_t, me_y, 1 - me_c), device_id_type=MESH,
        )

    def share(j, n):
        b = block[n]
        return pltpu.make_async_remote_copy(
            src_ref=grid_v.at[j, b], dst_ref=grid_v.at[j, b], send_sem=s_send.at[j, n], recv_sem=s_recv.at[j, n],
            device_id=at(me_t, me_y, 1 - me_c), device_id_type=MESH,
        )

    def pass_y(j, n):
        return pltpu.make_async_remote_copy(
            src_ref=grid_v.at[j, own], dst_ref=grid_v.at[j, own], send_sem=y_send.at[j, n],
            recv_sem=y_recv.at[j, n], device_id=at(me_t, (y_up, y_down)[n], me_c), device_id_type=MESH,
        )

    def forward(j, n):
        half = pl.ds(n * (PER // 2), PER // 2)
        b = block[1 + n]
        return pltpu.make_async_remote_copy(
            src_ref=grid_v.at[j, b, half], dst_ref=grid_v.at[j, b, half], send_sem=f_send.at[j, n],
            recv_sem=f_recv.at[j, n], device_id=at(me_t, (y_up, y_down)[n], me_c), device_id_type=MESH,
        )

    def gather(n, _):
        j = chunk(n)
        landed[j, me_t] = x16[x_rows(me_t, j), :]
        landed_all(j).wait_recv()
        for pair in range(PER // 2):
            both = landed[j, :, pair * 16:(pair + 1) * 16, :].astype(jnp.float32)
            for h in range(2):
                grid_v[j, own, 2 * pair + h] = (
                    both[:, h * 8:(h + 1) * 8, :].reshape(per_block, 128).astype(jnp.bfloat16)
                )
        pass_y(j, 0).start()
        pass_y(j, 1).start()
        share(j, 0).start()
        return 0

    lax.fori_loop(0, CH, gather, 0)

    m_hi = lax.shift_right_logical(m_row, 4).astype(jnp.float32)
    m_lo = (m_row & 15).astype(jnp.float32)
    split = jnp.concatenate([m_hi, m_lo, jnp.zeros((6, m_all), jnp.float32)], axis=0).astype(jnp.bfloat16)
    col = lax.broadcasted_iota(jnp.int32, (1, per_block), 1)
    slot_col = lax.shift_right_logical(col, 3) * (n_phi * slots) + (lax.shift_right_logical(col, 1) & 3)
    n_at = lax.broadcasted_iota(jnp.int32, (m_all, per_block), 0)
    part_at = (col & 1).astype(jnp.float32)
    q_at = (lax.broadcasted_iota(jnp.int32, (QP, 1), 0) + (me_p * PD - 1 + total)).astype(jnp.float32)

    def table(b, _):
        pick = (n_at == slot_col + b * slots).astype(jnp.bfloat16)
        moved = jnp.dot(split, pick, preferred_element_type=jnp.float32)
        m_col = moved[0:1, :] * 16.0 + moved[1:2, :]
        phase = wrap(m_col * q_at + (1.0 - part_at * 0.25) * total, total)
        table_v[b] = (turn_cos(phase, total) * (1.0 / math.sqrt(m_all))).astype(jnp.bfloat16)
        return 0

    lax.fori_loop(0, n_phi, table, 0)

    for r in reads[3:]:
        r.wait()
    index_v[0] = (cells_v[1] * QP + cells_v[0]) * 4
    index_v[1] = cells_v[2]
    to_smem = [pltpu.make_async_copy(index_v.at[n], dst, idx_sem.at[n]) for n, dst in enumerate((base_s, orient_s))]
    for copy in to_smem:
        copy.start()

    def relay(n, _):
        j = chunk(n)
        for h in range(2):
            pass_y(j, h).wait_recv()
            forward(j, h).start()
            share(j, 1 + h).start()
        return 0

    lax.fori_loop(0, CH, relay, 0)

    def halo(n):
        t = me_t + 1 if n == 0 else me_t + n_theta - 1
        return pltpu.make_async_remote_copy(
            src_ref=halo_out.at[n], dst_ref=halo_in.at[n], send_sem=h_send.at[n], recv_sem=h_recv.at[n],
            device_id=at(lax.rem(t, n_theta), me_y, me_c), device_id_type=MESH,
        )

    def put_taps(cell, b, rows_0, rows_1):
        for e, value in enumerate((rows_0, rows_1)):
            taps[pl.ds(cell * (QP * 4) + 2 * b + e, QP, stride=4), :] = value

    def finish(n):
        j = chunk(n)
        for h in range(4):
            share(j, h).wait_recv()

        def pair_of(pair, _):
            both = None
            for half in range(2):
                picked = [grid_v[j, pl.ds(half * (n_phi // 2), n_phi // 2), 2 * pair + h] for h in range(2)]
                right = jnp.concatenate([p.reshape(k_all // 2, 128) for p in picked], axis=1)
                left = jnp.concatenate([table_v[half * (n_phi // 2) + b] for b in range(n_phi // 2)], axis=1)
                term = jnp.dot(left, right, preferred_element_type=jnp.float32)
                both = term if both is None else both + term
            for h in range(2):
                r = j * PER + 2 * pair + h
                value = both[:, h * 128:(h + 1) * 128]
                turned = pltpu.roll(value, PSI - 1, 1)
                put_taps(r + 1, 0, value, turned)
                put_taps(r, 1, value, turned)

                @pl.when(r == RT - 1)
                def _():
                    halo_out[0] = value

                @pl.when(r == 0)
                def _():
                    halo_out[1] = value

            return 0

        lax.fori_loop(0, PER // 2, pair_of, 0)

        @pl.when(jnp.logical_and(n == 1, me_t < n_theta - 1))
        def _():
            halo(0).start()

        @pl.when(jnp.logical_and(n == 1, me_t > 0))
        def _():
            halo(1).start()

    def far(n, _):
        @pl.when(n < CH)
        def _():
            j = chunk(n)
            forward(j, 0).wait_recv()
            forward(j, 1).wait_recv()
            share(j, 3).start()

        @pl.when(n > 0)
        def _():
            finish(n - 1)

        return 0

    lax.fori_loop(0, CH + 1, far, 0)

    @pl.when(me_t > 0)
    def _():
        halo(0).wait_recv()

    @pl.when(me_t == 0)
    def _():
        halo_in[0] = jnp.zeros((QP, 128), jnp.float32)

    @pl.when(me_t < n_theta - 1)
    def _():
        halo(1).wait_recv()

    @pl.when(me_t == n_theta - 1)
    def _():
        halo_in[1] = jnp.zeros((QP, 128), jnp.float32)

    for n in range(2):
        value = halo_in[n]
        put_taps(n * RT, n, value, pltpu.roll(value, PSI - 1, 1))

    for copy in to_smem:
        copy.wait()
    lane = lax.broadcasted_iota(jnp.int32, (8, 128), 1)

    def group(g, _):
        picked = jnp.zeros((8, 128), jnp.float32)
        for n in range(128):
            eight = taps[pl.ds(base_s[g, n], 8), :]
            tap = jnp.sum(jnp.where(lane == orient_s[g, n], eight, 0.0), axis=1, keepdims=True)
            picked = jnp.where(lane == n, tap, picked)
        weights = weight_v[:, pl.ds(pl.multiple_of(g * 128, 128), 128)]
        out_ref[pl.ds(g, 1), :] = jnp.sum(picked * weights, axis=0, keepdims=True)
        return 0

    lax.fori_loop(0, groups, group, 0)

    @pl.when(me_t < n_theta - 1)
    def _():
        halo(0).wait_send()

    @pl.when(me_t > 0)
    def _():
        halo(1).wait_send()

    def drain(j, _):
        landed_all(j).wait_send()
        for h in range(2):
            pass_y(j, h).wait_send()
            forward(j, h).wait_send()
        for h in range(4):
            share(j, h).wait_send()
        return 0

    lax.fori_loop(0, CH, drain, 0)


def shards(
    alm, wig, slot_order, beam, phi_cell, theta_cell, orient_cell_index, tap_weight, sample_count
):
    n_theta, n_phi = lax.axis_size("theta"), lax.axis_size("phi")
    slots, _, ldeg = alm.shape
    m_all = slot_order.shape[0]
    tile = min(ldeg // 2, 4096)
    tiles = ldeg // tile
    k_block = n_theta * 2 * slots
    groups = phi_cell.shape[0] // 128
    cells = [c.reshape(groups, 128) for c in (phi_cell, theta_cell, orient_cell_index)]
    anywhere = pl.BlockSpec(memory_space=pl.ANY)
    dma = pltpu.SemaphoreType.DMA
    f32, bf16, i32 = jnp.float32, jnp.bfloat16, jnp.int32
    value = pl.pallas_call(
        functools.partial(kernel, n_theta, n_phi, slots, ldeg, tile, m_all, groups),
        out_shape=jax.ShapeDtypeStruct((groups, 128), f32),
        in_specs=[anywhere] * 8,
        out_specs=pl.BlockSpec(memory_space=pltpu.VMEM),
        scratch_shapes=[
            pltpu.VMEM((slots * tiles, wig.shape[1], tile), bf16),
            pltpu.VMEM(beam.shape, bf16),
            pltpu.VMEM((128, tile), bf16),
            pltpu.VMEM(alm.shape, bf16),
            pltpu.VMEM((1, m_all), i32),
            pltpu.VMEM((3, groups, 128), i32),
            pltpu.VMEM(tap_weight.shape, f32),
            pltpu.VMEM((256, 256), bf16),
            pltpu.VMEM((slots, 256, n_theta * RT), f32),
            pltpu.VMEM((n_theta * RT * 8, 128), f32),
            pltpu.VMEM((n_theta * RT * 8, 128), bf16),
            pltpu.VMEM((CH, n_theta, PER * 8, 128), bf16),
            pltpu.VMEM((CH, n_phi, PER, k_block, 128), bf16),
            pltpu.VMEM((n_phi, QP, k_block), bf16),
            pltpu.VMEM((2, QP, 128), f32),
            pltpu.VMEM((2, QP, 128), f32),
            pltpu.VMEM(((RT + 1) * QP * 4 + 8, 128), f32),
            pltpu.VMEM((2, groups, 128), i32),
            pltpu.SMEM((groups, 128), i32),
            pltpu.SMEM((groups, 128), i32),
            dma((slots * tiles,)), dma((7,)), dma((2,)),
            dma((CH,)), dma((CH,)),
            dma((CH, 2)), dma((CH, 2)),
            dma((CH, 2)), dma((CH, 2)),
            dma((CH, 4)), dma((CH, 4)),
            dma((2,)), dma((2,)),
        ],
        compiler_params=pltpu.CompilerParams(
            collective_id=0, has_side_effects=True, vmem_limit_bytes=58 << 20
        ),
        name="convolve",
    )(wig, alm, beam, slot_order.reshape(1, -1), *cells, tap_weight)
    live = jnp.arange(phi_cell.shape[0], dtype=jnp.int32) < sample_count[0]
    return jnp.where(live, value.reshape(-1), jnp.float32(0.0))


def solution(mesh):
    return jax.shard_map(
        shards,
        mesh=mesh,
        in_specs=(
            P(("theta", "phi"), None, None),
            P(("theta", "phi"), None, None),
            P(),
            P(),
            P(("theta", "phi")),
            P(("theta", "phi")),
            P(("theta", "phi")),
            P(None, ("theta", "phi")),
            P(("theta", "phi")),
        ),
        out_specs=P(("theta", "phi")),
        check_vma=False,
    )
```

time: 192 us -> 56.7 us (0.30)
  the two profiles are of different devices: /device:TPU:6 before, /device:TPU:1 now
where the time goes in v2:
time: 56.7 us; the launch traced here: 56.5 us
  Pallas kernels  54.5 us (96%)
  other arithmetic  1.33 us (2%)
  between operations  0.66 us (1%)
    pallas_call x1, Pallas kernels, shards(): pl.pallas_call(functools.partial(kernel, n_theta, n_phi, slots, ldeg, til...  54.5 us
    select_n x1, other arithmetic, shards(): return jnp.where(live, value.reshape(-1), jnp.float32(0.0))  1.33 us

profile of v2, /device:TPU:1, one launch (start us, length us, event | category | flops | bytes accessed | tf_op | source)
XLA Modules:
  0.0 56.5 jit_solution(10170106735746618851)
XLA Ops:
  0.7 54.5 %convolve.1 = f32[32,128]{1,0:T(8,128)} custom-call(bf16[4,256,8192]{2,1,0:T(8,128)(2,1)} %wig_hbm.1, bf16[4,2,8192]{2,1,0:T(2,128)(2,1)} %alm_hbm.1, bf16[8192,128]{1,0:T(8,128)(2,1)} %beam_hbm.1, s32[1,512]{1,0:T(1,128)} %bitcast.11, s32[32,128]{1,0:T(8,128)} %bitcast.8, s32[32,128]{1,0:T(8,128)} %bitcast.9, s32[32,128]{1,0:T(8,128)} %bitcast.10, ...), custom_call_target="tpu_custom_call" | custom-call | tf_op jit(solution)/shard_map/convolve/pallas_call | solution.py:417
  55.1 1.3 %bitcast_select_fusion = f32[4096]{0:T(1024)} fusion(f32[32,128]{1,0:T(8,128)} %convolve.1, s32[]{:T(128)} %bitcast.7), kind=kLoop, calls=%fused_computation | loop fusion | flops 8192 | bytes 32772 | tf_op jit(solution)/shard_map/jit(_where)/select_n | solution.py:456

commit v3 on v2

v3 whole, which is shorter than its diff:
```python
import functools
import math

import jax
import jax.numpy as jnp
from jax import lax
from jax.experimental import pallas as pl
from jax.experimental.pallas import tpu as pltpu
from jax.sharding import PartitionSpec as P

PSI = 128
PD = 192
RT = 16
QP = 208
HALF = RT // 2
MESH = pl.DeviceIdType.MESH
NT = (((1,), (1,)), ((), ()))
TN = (((0,), (0,)), ((), ()))


def slot_m(order, half, m_all):
    stride = max(half // m_all, 1)
    m = lax.shift_right_logical(order * half, m_all.bit_length() - 1)
    if stride > 1:
        m = m + (7 * order) % stride
    return m


def turn_cos(phase, total):
    x = (jnp.abs(phase - total / 2) - total / 4) * (2.0 * math.pi / total)
    x2 = x * x
    p = jnp.float32(-1.0 / math.factorial(11))
    for n in (9, 7, 5, 3, 1):
        p = p * x2 + jnp.float32((-1) ** (n // 2) / math.factorial(n))
    return p * x


def wrap(value, total):
    return value - jnp.floor((value + 0.5) * jnp.float32(1.0 / total)) * total


def psi_rows():
    k_at = lax.broadcasted_iota(jnp.int32, (128, 128), 0)
    p_at = lax.broadcasted_iota(jnp.int32, (128, 128), 1)
    turn = ((k_at * p_at) & (PSI - 1)).astype(jnp.float32)
    scale = 1.0 / math.sqrt(2 * 128)
    psi0 = turn_cos(turn, PSI) * scale
    psi1 = -turn_cos(wrap(turn + 0.75 * PSI, PSI), PSI) * scale
    return psi0.astype(jnp.bfloat16), psi1.astype(jnp.bfloat16), (-psi0).astype(jnp.bfloat16)


def kernel(
    n_theta, n_phi, slots, ldeg, tile, m_all, groups,
    wig_hbm, alm_hbm, beam_hbm, order_hbm, phi_hbm, theta_hbm, orient_hbm, weight_hbm, out_ref,
    wig_v, beam_v, beam_t, alm_v, order_v, cells_v, weight_v, psi_v, sums, x32, x16, landed, spread, grid_v,
    table_v, part_v, share_out, share_in, halo_out, halo_in, taps, index_v,
    base_s, orient_s, wig_sem, in_sem, idx_sem, a_send, a_recv, y_send, y_recv, f_send, f_recv, s_send, s_recv, h_send, h_recv,
):
    me_t = lax.axis_index("theta")
    me_p = lax.axis_index("phi")
    me_y, me_c = me_p // 2, me_p % 2
    n_y = n_phi // 2
    total = PD * n_phi
    tiles = ldeg // tile
    sources = 2 * n_theta
    span = HALF * 4
    per_block = 4 * sources
    pairs = HALF // 2
    y_up, y_down, y_far = (me_y + 1) % n_y, (me_y + n_y - 1) % n_y, (me_y + 2) % n_y

    def at(t, y, c):
        return (t, y * 2 + c)

    reads = [
        pltpu.make_async_copy(src, dst, in_sem.at[n])
        for n, (src, dst) in enumerate(
            (
                (beam_hbm, beam_v), (alm_hbm, alm_v), (order_hbm, order_v), (phi_hbm, cells_v.at[0]),
                (theta_hbm, cells_v.at[1]), (orient_hbm, cells_v.at[2]), (weight_hbm, weight_v),
            )
        )
    ]

    def place(n):
        sh, i, s2 = n // (2 * tiles), n // 2 % tiles, n % 2
        return sh * 2 + s2, i

    def wig_copy(n):
        s, i = place(n)
        return pltpu.make_async_copy(
            wig_hbm.at[s, :, pl.ds(pl.multiple_of(i * tile, 128), tile)], wig_v.at[n], wig_sem.at[n]
        )

    for r in reads[:3]:
        r.start()

    def wig_start(n, _):
        wig_copy(n).start()
        return 0

    lax.fori_loop(0, slots * tiles, wig_start, 0)
    for r in reads[3:]:
        r.start()

    def target(n):
        return (me_t + (n + 1) // 2) % n_theta, (me_c + n + 1) % 2

    barrier = pltpu.get_barrier_semaphore()

    def greet(n, _):
        t, c = target(n)
        pl.semaphore_signal(barrier, inc=1, device_id=at(t, me_y, c), device_id_type=MESH)
        return 0

    others = sources - 1
    lax.fori_loop(0, others, greet, 0)
    for y in (y_up, y_down):
        pl.semaphore_signal(barrier, inc=1, device_id=at(me_t, y, me_c), device_id_type=MESH)

    psi0, psi1, psi2 = psi_rows()
    psi_v[:128, :128] = psi0
    psi_v[:128, 128:] = psi1
    psi_v[128:, :128] = psi1
    psi_v[128:, 128:] = psi2
    for r in reads[:3]:
        r.wait()

    m_row = slot_m(order_v[...], total // 2, m_all)
    slot_lane = lax.broadcasted_iota(jnp.int32, (1, m_all), 1)
    eye = (
        lax.broadcasted_iota(jnp.int32, (128, 128), 0) == lax.broadcasted_iota(jnp.int32, (128, 128), 1)
    ).astype(jnp.bfloat16)

    def stage(n, _):
        s, i = place(n)

        @pl.when(jnp.logical_and(n < 2 * tiles, n % 2 == 0))
        def _():
            beam_t[i] = lax.dot_general(
                eye, beam_v[pl.ds(pl.multiple_of(i * tile, 128), tile), :], NT, preferred_element_type=jnp.float32
            ).astype(jnp.bfloat16)

        mine = slot_lane == (me_t * n_phi + me_p) * slots + s
        m_own = jnp.sum(jnp.where(mine, m_row, 0).astype(jnp.float32), axis=1, keepdims=True)
        degree = (lax.broadcasted_iota(jnp.int32, (2, tile), 1) + i * tile).astype(jnp.float32)
        sky = alm_v[s, :, pl.ds(pl.multiple_of(i * tile, 128), tile)].astype(jnp.float32)
        sky = jnp.where(degree >= m_own, sky, 0.0)
        weighted = jnp.concatenate(
            [
                beam_t[i] * jnp.broadcast_to(sky[c:c + 1, :], (128, tile)).astype(jnp.bfloat16)
                for c in range(2)
            ],
            axis=0,
        )
        wig_copy(n).wait()
        term = lax.dot_general(weighted, wig_v[n], NT, preferred_element_type=jnp.float32)

        @pl.when(i == 0)
        def _():
            sums[n % 2] = term

        @pl.when(i > 0)
        def _():
            sums[n % 2] += term

        return 0

    def quad_at(q, c):
        return q + c * (1 - 2 * q)

    def quad_rows(t, c, q):
        return pl.ds(pl.multiple_of((t * 2 + c) * span + quad_at(q, c) * 16, 16), 16)

    def send_half(sh, _):
        lax.fori_loop(sh * 2 * tiles, (sh + 1) * 2 * tiles, stage, 0)

        def to_psi(s2, _):
            x = lax.dot_general(sums[s2].astype(jnp.bfloat16), psi_v[...], TN, preferred_element_type=jnp.float32)
            for c in range(2):
                x32[pl.ds(2 * s2 + c, n_theta * RT, stride=4), :] = x[:, c * 128:(c + 1) * 128]
            return 0

        lax.fori_loop(0, 2, to_psi, 0)

        def narrow(n, _):
            rows = pl.ds(pl.multiple_of(n * RT * 4, 16), RT * 4)
            x16[sh, rows, :] = x32[rows, :].astype(jnp.bfloat16)
            return 0

        lax.fori_loop(0, n_theta, narrow, 0)

        @pl.when(sh == 0)
        def _():
            pl.semaphore_wait(barrier, others + 2)

        def send(n, _):
            q = n // others
            t, c = target(n % others)
            pltpu.make_async_remote_copy(
                src_ref=x16.at[sh, quad_rows(t, c, q), :], dst_ref=landed.at[sh, q, me_t * 2 + me_c],
                send_sem=a_send.at[sh, q], recv_sem=a_recv.at[sh, q],
                device_id=at(t, me_y, c), device_id_type=MESH,
            ).start()
            return 0

        lax.fori_loop(0, 2 * others, send, 0)
        for q in range(2):
            landed[sh, q, me_t * 2 + me_c] = x16[sh, quad_rows(me_t, me_c, q), :]
        return 0

    lax.fori_loop(0, 2, send_half, 0)

    def arrived(sh, q):
        block = landed.at[sh, q, pl.ds(0, others)]
        return pltpu.make_async_remote_copy(
            src_ref=block, dst_ref=block, send_sem=a_send.at[sh, q], recv_sem=a_recv.at[sh, q],
            device_id=at(me_t, me_y, 1 - me_c), device_id_type=MESH,
        )

    def pass_y(sh, q, h):
        block = grid_v.at[sh, me_y, pl.ds(quad_at(q, me_c) * 4, 4)]
        return pltpu.make_async_remote_copy(
            src_ref=block, dst_ref=block, send_sem=y_send.at[sh, q, h], recv_sem=y_recv.at[sh, q, h],
            device_id=at(me_t, (y_up, y_down)[h], me_c), device_id_type=MESH,
        )

    def forward(sh, q, h):
        block = grid_v.at[sh, (y_down, y_up)[h], pl.ds(quad_at(q, me_c) * 4 + 2 * h, 2)]
        return pltpu.make_async_remote_copy(
            src_ref=block, dst_ref=block, send_sem=f_send.at[sh, q, h], recv_sem=f_recv.at[sh, q, h],
            device_id=at(me_t, (y_up, y_down)[h], me_c), device_id_type=MESH,
        )

    def gather(sh, q):
        arrived(sh, q).wait_recv()
        spread[...] = landed[sh, q].astype(jnp.float32).reshape(sources * 16, 128)
        first = quad_at(q, me_c) * 4

        def cycle(r, _):
            for p in range(4):
                grid_v[sh, me_y, first + r, p * sources:(p + 1) * sources, :] = spread[
                    pl.ds(r * 4 + p, sources, stride=16), :
                ].astype(jnp.bfloat16)
            return 0

        lax.fori_loop(0, 4, cycle, 0)
        pass_y(sh, q, 0).start()
        pass_y(sh, q, 1).start()

    def relay(sh, q):
        for h in range(2):
            pass_y(sh, q, h).wait_recv()
            forward(sh, q, h).start()

    def far(sh, q):
        for h in range(2):
            forward(sh, q, h).wait_recv()

    gather(0, 0)
    gather(0, 1)

    m_hi = lax.shift_right_logical(m_row, 4).astype(jnp.float32)
    m_lo = (m_row & 15).astype(jnp.float32)
    split = jnp.concatenate([m_hi, m_lo, jnp.zeros((6, m_all), jnp.float32)], axis=0).astype(jnp.bfloat16)
    col = lax.broadcasted_iota(jnp.int32, (1, per_block), 1)
    part = col // sources
    source = col % sources
    slot_col = (source // 2 * n_phi + source % 2) * slots + part // 2
    n_at = lax.broadcasted_iota(jnp.int32, (m_all, per_block), 0)
    part_at = (part % 2).astype(jnp.float32)
    row = lax.broadcasted_iota(jnp.int32, (2 * QP, 1), 0)
    sibling = me_y * 2 + 1 - me_c
    q_at = jnp.where(row < QP, row + me_p * PD, row - QP + sibling * PD) - 1 + total
    q_at = q_at.astype(jnp.float32)

    def table(n, _):
        sh, b = n // n_y, n % n_y
        pick = (n_at == slot_col + (b * 2 * slots + sh * 2)).astype(jnp.bfloat16)
        moved = jnp.dot(split, pick, preferred_element_type=jnp.float32)
        m_col = moved[0:1, :] * 16.0 + moved[1:2, :]
        phase = wrap(m_col * q_at + (1.0 - part_at * 0.25) * total, total)
        table_v[sh, :, pl.ds(pl.multiple_of(b * per_block, per_block), per_block)] = (
            turn_cos(phase, total) * (1.0 / math.sqrt(m_all))
        ).astype(jnp.bfloat16)
        return 0

    lax.fori_loop(0, 2 * n_y, table, 0)

    for r in reads[3:]:
        r.wait()
    index_v[0] = (cells_v[1] * QP + cells_v[0]) * 4
    index_v[1] = cells_v[2]
    to_smem = [pltpu.make_async_copy(index_v.at[n], dst, idx_sem.at[n]) for n, dst in enumerate((base_s, orient_s))]
    for copy in to_smem:
        copy.start()

    def product(sh, pair):
        right = jnp.concatenate(
            [grid_v[sh, :, 2 * pair + h].reshape(n_y * per_block, 128) for h in range(2)], axis=1
        )
        return jnp.dot(table_v[sh], right, preferred_element_type=jnp.float32)

    relay(0, 0)
    gather(1, 0)
    relay(0, 1)
    gather(1, 1)

    def first_part(pair, _):
        part_v[pair] = product(0, pair)
        return 0

    far(0, 0)
    far(0, 1)
    relay(1, 0)
    lax.fori_loop(0, pairs // 2, first_part, 0)
    relay(1, 1)
    lax.fori_loop(pairs // 2, pairs, first_part, 0)

    def share(n):
        return pltpu.make_async_remote_copy(
            src_ref=share_out.at[n], dst_ref=share_in.at[n], send_sem=s_send.at[n], recv_sem=s_recv.at[n],
            device_id=at(me_t, me_y, 1 - me_c), device_id_type=MESH,
        )

    def halo(n):
        t = (me_t + n_theta - 1 + 2 * me_c) % n_theta
        return pltpu.make_async_remote_copy(
            src_ref=halo_out.at[n], dst_ref=halo_in.at[1 - me_c], send_sem=h_send.at[n], recv_sem=h_recv.at[1 - me_c],
            device_id=at(t, me_y, (me_c + n) % 2), device_id_type=MESH,
        )

    edge_goes = jnp.logical_or(
        jnp.logical_and(me_c == 0, me_t > 0), jnp.logical_and(me_c == 1, me_t < n_theta - 1)
    )

    def put_taps(cell, b, value):
        for e, rows in enumerate((value, pltpu.roll(value, PSI - 1, 1))):
            taps[pl.ds(cell * (QP * 4) + 2 * b + e, QP, stride=4), :] = rows

    def put_cycle(r, value):
        turned = pltpu.roll(value, PSI - 1, 1)
        for cell, b in ((r + 1, 0), (r, 1)):
            for e, rows in enumerate((value, turned)):
                taps[pl.ds(cell * (QP * 4) + 2 * b + e, QP, stride=4), :] = rows

    def pair_at(n, c):
        return n + c * (pairs - 1 - 2 * n)

    def finish(n, _):
        pair = pair_at(n, me_c)

        @pl.when(n % 2 == 0)
        def _():
            far(1, n // 2)

        both = product(1, pair) + part_v[pair]
        for h in range(2):
            share_out[n, h] = both[QP:, h * 128:(h + 1) * 128].astype(jnp.bfloat16)
        share(n).start()

        @pl.when(n == 0)
        def _():
            for i in range(2):
                rows = both[i * QP:(i + 1) * QP]
                halo_out[i] = jnp.where(me_c == 0, rows[:, :128], rows[:, 128:]).astype(jnp.bfloat16)

        @pl.when(jnp.logical_and(n == 0, edge_goes))
        def _():
            halo(0).start()
            halo(1).start()

        for h in range(2):
            put_cycle(me_c * HALF + 2 * pair + h, both[:QP, h * 128:(h + 1) * 128])
        return 0

    lax.fori_loop(0, pairs, finish, 0)

    def take_share(n, _):
        share(n).wait_recv()
        for h in range(2):
            put_cycle((1 - me_c) * HALF + 2 * pair_at(n, 1 - me_c) + h, share_in[n, h].astype(jnp.float32))
        return 0

    lax.fori_loop(0, pairs, take_share, 0)

    def edge_in(slot):
        return pltpu.make_async_remote_copy(
            src_ref=halo_out.at[0], dst_ref=halo_in.at[slot], send_sem=h_send.at[0], recv_sem=h_recv.at[slot],
            device_id=at(me_t, me_y, 1 - me_c), device_id_type=MESH,
        )

    for slot, at_end in ((0, me_t == 0), (1, me_t == n_theta - 1)):
        @pl.when(jnp.logical_not(at_end))
        def _():
            edge_in(slot).wait_recv()

        @pl.when(at_end)
        def _():
            halo_in[slot] = jnp.zeros((QP, 128), jnp.bfloat16)

        put_taps(slot * RT, slot, halo_in[slot].astype(jnp.float32))

    for copy in to_smem:
        copy.wait()
    lane = lax.broadcasted_iota(jnp.int32, (8, 128), 1)

    def group(g, _):
        picked = jnp.zeros((8, 128), jnp.float32)
        for n in range(128):
            eight = taps[pl.ds(base_s[g, n], 8), :]
            tap = jnp.sum(jnp.where(lane == orient_s[g, n], eight, 0.0), axis=1, keepdims=True)
            picked = jnp.where(lane == n, tap, picked)
        weights = weight_v[:, pl.ds(pl.multiple_of(g * 128, 128), 128)]
        out_ref[pl.ds(g, 1), :] = jnp.sum(picked * weights, axis=0, keepdims=True)
        return 0

    lax.fori_loop(0, groups, group, 0)

    @pl.when(edge_goes)
    def _():
        halo(0).wait_send()
        halo(1).wait_send()

    def drain(sh, _):
        for q in range(2):
            arrived(sh, q).wait_send()
            for h in range(2):
                pass_y(sh, q, h).wait_send()
                forward(sh, q, h).wait_send()
        return 0

    lax.fori_loop(0, 2, drain, 0)

    def drain_share(n, _):
        share(n).wait_send()
        return 0

    lax.fori_loop(0, pairs, drain_share, 0)


def shards(
    alm, wig, slot_order, beam, phi_cell, theta_cell, orient_cell_index, tap_weight, sample_count
):
    n_theta, n_phi = lax.axis_size("theta"), lax.axis_size("phi")
    slots, _, ldeg = alm.shape
    m_all = slot_order.shape[0]
    tile = min(ldeg // 2, 4096)
    tiles = ldeg // tile
    n_y = n_phi // 2
    sources = 2 * n_theta
    block = 4 * sources
    pairs = HALF // 2
    groups = phi_cell.shape[0] // 128
    cells = [c.reshape(groups, 128) for c in (phi_cell, theta_cell, orient_cell_index)]
    anywhere = pl.BlockSpec(memory_space=pl.ANY)
    dma = pltpu.SemaphoreType.DMA
    f32, bf16, i32 = jnp.float32, jnp.bfloat16, jnp.int32
    value = pl.pallas_call(
        functools.partial(kernel, n_theta, n_phi, slots, ldeg, tile, m_all, groups),
        out_shape=jax.ShapeDtypeStruct((groups, 128), f32),
        in_specs=[anywhere] * 8,
        out_specs=pl.BlockSpec(memory_space=pltpu.VMEM),
        scratch_shapes=[
            pltpu.VMEM((slots * tiles, wig.shape[1], tile), bf16),
            pltpu.VMEM(beam.shape, bf16),
            pltpu.VMEM((tiles, 128, tile), bf16),
            pltpu.VMEM(alm.shape, bf16),
            pltpu.VMEM((1, m_all), i32),
            pltpu.VMEM((3, groups, 128), i32),
            pltpu.VMEM(tap_weight.shape, f32),
            pltpu.VMEM((256, 256), bf16),
            pltpu.VMEM((2, 256, n_theta * RT), f32),
            pltpu.VMEM((n_theta * RT * 4, 128), f32),
            pltpu.VMEM((2, n_theta * RT * 4, 128), bf16),
            pltpu.VMEM((2, 2, sources, 16, 128), bf16),
            pltpu.VMEM((sources * 16, 128), f32),
            pltpu.VMEM((2, n_y, HALF, block, 128), bf16),
            pltpu.VMEM((2, 2 * QP, n_y * block), bf16),
            pltpu.VMEM((pairs, 2 * QP, 256), f32),
            pltpu.VMEM((pairs, 2, QP, 128), bf16),
            pltpu.VMEM((pairs, 2, QP, 128), bf16),
            pltpu.VMEM((2, QP, 128), bf16),
            pltpu.VMEM((2, QP, 128), bf16),
            pltpu.VMEM(((RT + 1) * QP * 4 + 8, 128), f32),
            pltpu.VMEM((2, groups, 128), i32),
            pltpu.SMEM((groups, 128), i32),
            pltpu.SMEM((groups, 128), i32),
            dma((slots * tiles,)), dma((7,)), dma((2,)),
            dma((2, 2)), dma((2, 2)),
            dma((2, 2, 2)), dma((2, 2, 2)),
            dma((2, 2, 2)), dma((2, 2, 2)),
            dma((pairs,)), dma((pairs,)),
            dma((2,)), dma((2,)),
        ],
        compiler_params=pltpu.CompilerParams(
            collective_id=0, has_side_effects=True, vmem_limit_bytes=58 << 20
        ),
        name="convolve",
    )(wig, alm, beam, slot_order.reshape(1, -1), *cells, tap_weight)
    live = jnp.arange(phi_cell.shape[0], dtype=jnp.int32) < sample_count[0]
    return jnp.where(live, value.reshape(-1), jnp.float32(0.0))


def solution(mesh):
    return jax.shard_map(
        shards,
        mesh=mesh,
        in_specs=(
            P(("theta", "phi"), None, None),
            P(("theta", "phi"), None, None),
            P(),
            P(),
            P(("theta", "phi")),
            P(("theta", "phi")),
            P(("theta", "phi")),
            P(None, ("theta", "phi")),
            P(("theta", "phi")),
        ),
        out_specs=P(("theta", "phi")),
        check_vma=False,
    )
```

time: 56.7 us -> 52.4 us (0.924)
  Pallas kernels: 54.5 us -> 50.2 us
    pallas_call x1, Pallas kernels: 54.5 us -> 50.2 us  [shards(): pl.pallas_call(functools.partial(kernel, n_theta, n_phi, slots, ldeg, til...]
where the time goes in v3:
time: 52.4 us; the launch traced here: 52.2 us
  Pallas kernels  50.2 us (96%)
  other arithmetic  1.33 us (3%)
  between operations  0.66 us (1%)
    pallas_call x1, Pallas kernels, shards(): pl.pallas_call(functools.partial(kernel, n_theta, n_phi, slots, ldeg, til...  50.2 us
    select_n x1, other arithmetic, shards(): return jnp.where(live, value.reshape(-1), jnp.float32(0.0))  1.33 us

profile of v3, /device:TPU:1, one launch (start us, length us, event | category | flops | bytes accessed | tf_op | source)
XLA Modules:
  0.0 52.2 jit_solution(9768951659735719303)
XLA Ops:
  0.7 50.2 %convolve.1 = f32[32,128]{1,0:T(8,128)} custom-call(bf16[4,256,8192]{2,1,0:T(8,128)(2,1)} %wig_hbm.1, bf16[4,2,8192]{2,1,0:T(2,128)(2,1)} %alm_hbm.1, bf16[8192,128]{1,0:T(8,128)(2,1)} %beam_hbm.1, s32[1,512]{1,0:T(1,128)} %bitcast.11, s32[32,128]{1,0:T(8,128)} %bitcast.8, s32[32,128]{1,0:T(8,128)} %bitcast.9, s32[32,128]{1,0:T(8,128)} %bitcast.10, ...), custom_call_target="tpu_custom_call" | custom-call | tf_op jit(solution)/shard_map/convolve/pallas_call | solution.py:458
  50.9 1.3 %bitcast_select_fusion = f32[4096]{0:T(1024)} fusion(f32[32,128]{1,0:T(8,128)} %convolve.1, s32[]{:T(128)} %bitcast.7), kind=kLoop, calls=%fused_computation | loop fusion | flops 8192 | bytes 32772 | tf_op jit(solution)/shard_map/jit(_where)/select_n | solution.py:501

commit v4 on v3

v4 whole, which is shorter than its diff:
```python
import functools
import math

import jax
import jax.numpy as jnp
from jax import lax
from jax.experimental import pallas as pl
from jax.experimental.pallas import tpu as pltpu
from jax.sharding import PartitionSpec as P

PSI = 128
PD = 192
RT = 16
QP = 208
HALF = RT // 2
MESH = pl.DeviceIdType.MESH
NT = (((1,), (1,)), ((), ()))


def slot_m(order, half, m_all):
    stride = max(half // m_all, 1)
    m = lax.shift_right_logical(order * half, m_all.bit_length() - 1)
    if stride > 1:
        m = m + (7 * order) % stride
    return m


def turn_cos(phase, total):
    x = (jnp.abs(phase - total / 2) - total / 4) * (2.0 * math.pi / total)
    x2 = x * x
    p = jnp.float32(-1.0 / math.factorial(11))
    for n in (9, 7, 5, 3, 1):
        p = p * x2 + jnp.float32((-1) ** (n // 2) / math.factorial(n))
    return p * x


def wrap(value, total):
    return value - jnp.floor((value + 0.5) * jnp.float32(1.0 / total)) * total


def psi_rows():
    k_at = lax.broadcasted_iota(jnp.int32, (128, 128), 0)
    p_at = lax.broadcasted_iota(jnp.int32, (128, 128), 1)
    turn = ((k_at * p_at) & (PSI - 1)).astype(jnp.float32)
    scale = 1.0 / math.sqrt(2 * 128)
    psi0 = turn_cos(turn, PSI) * scale
    psi1 = -turn_cos(wrap(turn + 0.75 * PSI, PSI), PSI) * scale
    return psi0.astype(jnp.bfloat16), psi1.astype(jnp.bfloat16), (-psi0).astype(jnp.bfloat16)


def kernel(
    n_theta, n_phi, slots, ldeg, tile, m_all, groups,
    wig_hbm, alm_hbm, beam_hbm, order_hbm, phi_hbm, theta_hbm, orient_hbm, weight_hbm, count_hbm, out_ref,
    wig_v, beam_v, beam_t, alm_v, sky_v, order_v, cells_v, weight_v, psi_v, sums, x32, x16, landed, spread, grid_v,
    table_v, part_v, share_out, share_in, halo_out, halo_in, taps, index_v,
    base_s, orient_s, count_s, wig_sem, beam_sem, in_sem, idx_sem, a_send, a_recv, y_send, y_recv, f_send, f_recv, s_send, s_recv, h_send, h_recv,
):
    me_t = lax.axis_index("theta")
    me_p = lax.axis_index("phi")
    me_y, me_c = me_p // 2, me_p % 2
    n_y = n_phi // 2
    total = PD * n_phi
    tiles = ldeg // tile
    sources = 2 * n_theta
    bunch = sources // 4
    span = HALF * 4
    per_block = 4 * bunch
    wide = n_y * per_block
    pairs = HALF // 2
    y_up, y_down, y_far = (me_y + 1) % n_y, (me_y + n_y - 1) % n_y, (me_y + 2) % n_y

    def at(t, y, c):
        return (t, y * 2 + c)

    reads = [
        pltpu.make_async_copy(src, dst, in_sem.at[n])
        for n, (src, dst) in enumerate(
            (
                (alm_hbm, alm_v), (order_hbm, order_v), (count_hbm, count_s), (phi_hbm, cells_v.at[0]),
                (theta_hbm, cells_v.at[1]), (orient_hbm, cells_v.at[2]), (weight_hbm, weight_v),
            )
        )
    ]

    def place(n):
        sh, i, s2 = n // (2 * tiles), n // 2 % tiles, n % 2
        return sh * 2 + s2, i

    def wig_copy(n):
        s, i = place(n)
        return pltpu.make_async_copy(
            wig_hbm.at[s, :, pl.ds(pl.multiple_of(i * tile, 128), tile)], wig_v.at[n], wig_sem.at[n]
        )

    def beam_copy(i):
        part = pl.ds(pl.multiple_of(i * tile, 128), tile)
        return pltpu.make_async_copy(beam_hbm.at[part, :], beam_v.at[part, :], beam_sem.at[i])

    for r in reads[:2]:
        r.start()
    for i in range(tiles):
        beam_copy(i).start()

    def wig_start(n, _):
        wig_copy(n).start()
        return 0

    lax.fori_loop(0, 2 * tiles, wig_start, 0)
    for r in reads[2:]:
        r.start()

    def target(n):
        m = n + 5 * sources // 8
        return (me_t + m // 2) & (n_theta - 1), (me_c + m) & 1

    barrier = pltpu.get_barrier_semaphore()

    def greet(n, _):
        t, c = target(n)

        @pl.when(n != alone)
        def _():
            pl.semaphore_signal(barrier, inc=1, device_id=at(t, me_y, c), device_id_type=MESH)

        return 0

    others = sources - 1
    alone = sources - 5 * sources // 8
    lax.fori_loop(0, sources, greet, 0)
    for y in (y_up, y_down):
        pl.semaphore_signal(barrier, inc=1, device_id=at(me_t, y, me_c), device_id_type=MESH)

    psi0, psi1, psi2 = psi_rows()
    psi_v[:128, :128] = psi0
    psi_v[:128, 128:] = psi1
    psi_v[128:, :128] = psi1
    psi_v[128:, 128:] = psi2
    for r in reads[:2]:
        r.wait()

    m_row = slot_m(order_v[...], total // 2, m_all)
    slot_lane = lax.broadcasted_iota(jnp.int32, (1, m_all), 1)
    eye = (
        lax.broadcasted_iota(jnp.int32, (128, 128), 0) == lax.broadcasted_iota(jnp.int32, (128, 128), 1)
    ).astype(jnp.bfloat16)

    m_hi = lax.shift_right_logical(m_row, 4).astype(jnp.float32)
    m_lo = (m_row & 15).astype(jnp.float32)
    split = jnp.concatenate([m_hi, m_lo, jnp.zeros((6, m_all), jnp.float32)], axis=0).astype(jnp.bfloat16)
    col = lax.broadcasted_iota(jnp.int32, (1, wide), 1)
    part = col % per_block // bunch
    source = col % bunch
    slot_col = (source // 2 * n_phi + col // per_block * 2 + source % 2) * slots + part // 2
    n_at = lax.broadcasted_iota(jnp.int32, (m_all, wide), 0)
    part_at = (part % 2).astype(jnp.float32)
    row = lax.broadcasted_iota(jnp.int32, (2 * QP, 1), 0)
    sibling = me_y * 2 + 1 - me_c
    q_at = jnp.where(row < QP, row + me_p * PD, row - QP + sibling * PD) - 1 + total
    q_at = q_at.astype(jnp.float32)

    def table(n, _):
        sh, g = n // 4, n % 4
        first = g * (n_theta // 4) * n_phi * slots + sh * 2
        pick = (n_at == slot_col + first).astype(jnp.bfloat16)
        moved = jnp.dot(split, pick, preferred_element_type=jnp.float32)
        m_col = moved[0:1, :] * 16.0 + moved[1:2, :]
        phase = wrap(m_col * q_at + (1.0 - part_at * 0.25) * total, total)
        table_v[sh, :, pl.ds(pl.multiple_of(g * wide, wide), wide)] = (
            turn_cos(phase, total) * (1.0 / math.sqrt(m_all))
        ).astype(jnp.bfloat16)
        return 0

    def turn_beam(i, _):
        beam_copy(i).wait()
        beam_t[i] = lax.dot_general(
            eye, beam_v[pl.ds(pl.multiple_of(i * tile, 128), tile), :], NT, preferred_element_type=jnp.float32
        ).astype(jnp.bfloat16)
        return 0

    def mask_sky(s, _):
        mine = slot_lane == (me_t * n_phi + me_p) * slots + s
        m_own = jnp.sum(jnp.where(mine, m_row, 0).astype(jnp.float32), axis=1, keepdims=True)
        degree = lax.broadcasted_iota(jnp.int32, (2, ldeg), 1).astype(jnp.float32)
        sky = jnp.where(degree >= m_own, alm_v[s].astype(jnp.float32), 0.0)
        for c in range(2):
            sky_v[s, c] = jnp.broadcast_to(sky[c:c + 1, :], (16, ldeg)).astype(jnp.bfloat16)
        return 0

    lax.fori_loop(0, slots, mask_sky, 0)
    lax.fori_loop(0, tiles, turn_beam, 0)

    def stage(n, _):
        s, i = place(n)
        part = beam_t[i].reshape(8, 16, tile)
        span_i = pl.ds(pl.multiple_of(i * tile, 128), tile)
        weighted = jnp.concatenate(
            [(part * sky_v[s, c, :, span_i][None]).reshape(128, tile) for c in range(2)], axis=0
        )
        wig_copy(n).wait()

        @pl.when(n < (slots - 2) * tiles)
        def _():
            wig_copy(n + 2 * tiles).start()

        term = lax.dot_general(wig_v[n], weighted, NT, preferred_element_type=jnp.float32)

        @pl.when(i == 0)
        def _():
            sums[n % 2] = term

        @pl.when(i > 0)
        def _():
            sums[n % 2] += term

        return 0

    def rows_of(t, c):
        return pl.ds(pl.multiple_of((t * 2 + c) * span, 16), span)

    def send_half(sh):
        def to_psi(s2, _):
            x = jnp.dot(sums[s2].astype(jnp.bfloat16), psi_v[...], preferred_element_type=jnp.float32)
            for c in range(2):
                x32[pl.ds(2 * s2 + c, n_theta * RT, stride=4), :] = x[:, c * 128:(c + 1) * 128]
            return 0

        lax.fori_loop(0, 2, to_psi, 0)

        x16[sh] = x32[...].astype(jnp.bfloat16)

        if sh == 0:
            pl.semaphore_wait(barrier, others + 2)

        def send(n, _):
            t, c = target(n)

            @pl.when(n != alone)
            def _():
                pltpu.make_async_remote_copy(
                    src_ref=x16.at[sh, rows_of(t, c), :], dst_ref=landed.at[sh, me_t * 2 + me_c],
                    send_sem=a_send.at[sh], recv_sem=a_recv.at[sh, me_t // (n_theta // 4)],
                    device_id=at(t, me_y, c), device_id_type=MESH,
                ).start()

            return 0

        lax.fori_loop(0, sources, send, 0)
        landed[sh, me_t * 2 + me_c] = x16[sh, rows_of(me_t, me_c), :]

    def arrived(sh, g, count):
        block = landed.at[sh, pl.ds(0, count)]
        return pltpu.make_async_remote_copy(
            src_ref=block, dst_ref=block, send_sem=a_send.at[sh], recv_sem=a_recv.at[sh, g],
            device_id=at(me_t, me_y, 1 - me_c), device_id_type=MESH,
        )

    def pass_y(sh, g, h):
        block = grid_v.at[sh, g, me_y]
        return pltpu.make_async_remote_copy(
            src_ref=block, dst_ref=block, send_sem=y_send.at[sh, g, h], recv_sem=y_recv.at[sh, g, h],
            device_id=at(me_t, (y_up, y_down)[h], me_c), device_id_type=MESH,
        )

    def forward(sh, g, h):
        block = grid_v.at[sh, g, (y_down, y_up)[h], pl.ds(h * (HALF // 2), HALF // 2)]
        return pltpu.make_async_remote_copy(
            src_ref=block, dst_ref=block, send_sem=f_send.at[sh, g, h], recv_sem=f_recv.at[sh, g, h],
            device_id=at(me_t, (y_up, y_down)[h], me_c), device_id_type=MESH,
        )

    own_bunch = me_t // (n_theta // 4)

    def gather(sh, g):
        @pl.when(g == own_bunch)
        def _():
            arrived(sh, g, bunch - 1).wait_recv()

        @pl.when(g != own_bunch)
        def _():
            arrived(sh, g, bunch).wait_recv()

        spread[...] = landed[sh, pl.ds(g * bunch, bunch)].astype(jnp.float32).reshape(bunch * span, 128)
        for r in range(HALF):
            grid_v[sh, g, me_y, r] = jnp.concatenate(
                [spread[pl.ds(r * 4 + p, bunch, stride=span), :] for p in range(4)], axis=0
            ).astype(jnp.bfloat16)
        pass_y(sh, g, 0).start()
        pass_y(sh, g, 1).start()

    def relay(sh, g):
        for h in range(2):
            pass_y(sh, g, h).wait_recv()
            forward(sh, g, h).start()

    def far(sh, g):
        for h in range(2):
            forward(sh, g, h).wait_recv()

    lax.fori_loop(0, 2 * tiles, stage, 0)
    send_half(0)
    lax.fori_loop(2 * tiles, 4 * tiles, stage, 0)
    gather(0, 0)
    send_half(1)

    for r in reads[2:]:
        r.wait()
    index_v[0] = (cells_v[1] * QP + cells_v[0]) * 4
    index_v[1] = cells_v[2]
    to_smem = [pltpu.make_async_copy(index_v.at[n], dst, idx_sem.at[n]) for n, dst in enumerate((base_s, orient_s))]
    for copy in to_smem:
        copy.start()

    def product(sh, bunches, pair):
        count = bunches.stop - bunches.start
        right = jnp.concatenate(
            [grid_v[sh, bunches, :, 2 * pair + h].reshape(count * wide, 128) for h in range(2)], axis=1
        )
        left = table_v[sh, :, bunches.start * wide:bunches.stop * wide]
        return jnp.dot(left, right, preferred_element_type=jnp.float32)

    def first_part(pair, _):
        part_v[pair] = product(0, slice(0, 4), pair)
        return 0

    def second_part(pair, _):
        part_v[pair] += product(1, slice(0, 3), pair)
        return 0

    def step(n, _):
        @pl.when(n == 4)
        def _():
            lax.fori_loop(0, 8, table, 0)

        @pl.when(n < 8)
        def _():
            gather(n // 4, n % 4)

        @pl.when(n >= 3)
        def _():
            relay((n - 3) // 4, (n - 3) % 4)

        return 0

    lax.fori_loop(1, 11, step, 0)
    for g in range(4):
        far(0, g)
    lax.fori_loop(0, pairs, first_part, 0)
    for g in range(3):
        far(1, g)
    lax.fori_loop(0, pairs, second_part, 0)

    def share(n):
        return pltpu.make_async_remote_copy(
            src_ref=share_out.at[n], dst_ref=share_in.at[n], send_sem=s_send.at[n], recv_sem=s_recv.at[n],
            device_id=at(me_t, me_y, 1 - me_c), device_id_type=MESH,
        )

    def halo(n):
        t = (me_t + n_theta - 1 + 2 * me_c) % n_theta
        return pltpu.make_async_remote_copy(
            src_ref=halo_out.at[n], dst_ref=halo_in.at[1 - me_c], send_sem=h_send.at[n], recv_sem=h_recv.at[1 - me_c],
            device_id=at(t, me_y, (me_c + n) % 2), device_id_type=MESH,
        )

    edge_goes = jnp.logical_or(
        jnp.logical_and(me_c == 0, me_t > 0), jnp.logical_and(me_c == 1, me_t < n_theta - 1)
    )

    def put_taps(cell, b, value):
        for e, rows in enumerate((value, pltpu.roll(value, PSI - 1, 1))):
            taps[pl.ds(cell * (QP * 4) + 2 * b + e, QP, stride=4), :] = rows

    def put_cycle(r, value):
        turned = pltpu.roll(value, PSI - 1, 1)
        for cell, b in ((r + 1, 0), (r, 1)):
            for e, rows in enumerate((value, turned)):
                taps[pl.ds(cell * (QP * 4) + 2 * b + e, QP, stride=4), :] = rows

    def pair_at(n, c):
        return n + c * (pairs - 1 - 2 * n)

    def finish(n, _):
        pair = pair_at(n, me_c)

        both = product(1, slice(3, 4), pair) + part_v[pair]
        for h in range(2):
            share_out[n, h] = both[QP:, h * 128:(h + 1) * 128].astype(jnp.bfloat16)
        share(n).start()

        @pl.when(n == 0)
        def _():
            for i in range(2):
                rows = both[i * QP:(i + 1) * QP]
                halo_out[i] = jnp.where(me_c == 0, rows[:, :128], rows[:, 128:]).astype(jnp.bfloat16)

        @pl.when(jnp.logical_and(n == 0, edge_goes))
        def _():
            halo(0).start()
            halo(1).start()

        part_v[pair, :QP] = both[:QP]
        return 0

    def put_own(pair, _):
        for h in range(2):
            put_cycle(me_c * HALF + 2 * pair + h, part_v[pair, :QP, h * 128:(h + 1) * 128])
        return 0

    far(1, 3)
    lax.fori_loop(0, pairs, finish, 0)
    lax.fori_loop(0, pairs, put_own, 0)

    def take_share(n, _):
        share(n).wait_recv()
        for h in range(2):
            put_cycle((1 - me_c) * HALF + 2 * pair_at(n, 1 - me_c) + h, share_in[n, h].astype(jnp.float32))
        return 0

    lax.fori_loop(0, pairs, take_share, 0)

    def edge_in(slot):
        return pltpu.make_async_remote_copy(
            src_ref=halo_out.at[0], dst_ref=halo_in.at[slot], send_sem=h_send.at[0], recv_sem=h_recv.at[slot],
            device_id=at(me_t, me_y, 1 - me_c), device_id_type=MESH,
        )

    for slot, at_end in ((0, me_t == 0), (1, me_t == n_theta - 1)):
        @pl.when(jnp.logical_not(at_end))
        def _():
            edge_in(slot).wait_recv()

        @pl.when(at_end)
        def _():
            halo_in[slot] = jnp.zeros((QP, 128), jnp.bfloat16)

        put_taps(slot * RT, slot, halo_in[slot].astype(jnp.float32))

    for copy in to_smem:
        copy.wait()
    lane = lax.broadcasted_iota(jnp.int32, (8, 128), 1)

    count = count_s[0]

    def group(g, _):
        picked = jnp.zeros((8, 128), jnp.float32)
        for n in range(128):
            eight = taps[pl.ds(base_s[g, n], 8), :]
            tap = jnp.sum(jnp.where(lane == orient_s[g, n], eight, 0.0), axis=1, keepdims=True)
            picked = jnp.where(lane == n, tap, picked)
        weights = weight_v[:, pl.ds(pl.multiple_of(g * 128, 128), 128)]
        value = jnp.sum(picked * weights, axis=0, keepdims=True)
        out_ref[pl.ds(g, 1), :] = jnp.where(lane[0:1, :] + g * 128 < count, value, 0.0)
        return 0

    lax.fori_loop(0, groups, group, 0)

    @pl.when(edge_goes)
    def _():
        halo(0).wait_send()
        halo(1).wait_send()

    def drain(sh, _):
        arrived(sh, 0, others).wait_send()
        for g in range(4):
            for h in range(2):
                pass_y(sh, g, h).wait_send()
                forward(sh, g, h).wait_send()
        return 0

    lax.fori_loop(0, 2, drain, 0)

    def drain_share(n, _):
        share(n).wait_send()
        return 0

    lax.fori_loop(0, pairs, drain_share, 0)


def shards(
    alm, wig, slot_order, beam, phi_cell, theta_cell, orient_cell_index, tap_weight, sample_count
):
    n_theta, n_phi = lax.axis_size("theta"), lax.axis_size("phi")
    slots, _, ldeg = alm.shape
    m_all = slot_order.shape[0]
    tile = min(ldeg // 2, 4096)
    tiles = ldeg // tile
    n_y = n_phi // 2
    sources = 2 * n_theta
    block = sources
    pairs = HALF // 2
    groups = phi_cell.shape[0] // 128
    cells = [c.reshape(groups, 128) for c in (phi_cell, theta_cell, orient_cell_index)]
    anywhere = pl.BlockSpec(memory_space=pl.ANY)
    dma = pltpu.SemaphoreType.DMA
    f32, bf16, i32 = jnp.float32, jnp.bfloat16, jnp.int32
    value = pl.pallas_call(
        functools.partial(kernel, n_theta, n_phi, slots, ldeg, tile, m_all, groups),
        out_shape=jax.ShapeDtypeStruct((groups, 128), f32),
        in_specs=[anywhere] * 9,
        out_specs=pl.BlockSpec(memory_space=pltpu.VMEM),
        scratch_shapes=[
            pltpu.VMEM((slots * tiles, wig.shape[1], tile), bf16),
            pltpu.VMEM(beam.shape, bf16),
            pltpu.VMEM((tiles, 128, tile), bf16),
            pltpu.VMEM(alm.shape, bf16),
            pltpu.VMEM((slots, 2, 16, ldeg), bf16),
            pltpu.VMEM((1, m_all), i32),
            pltpu.VMEM((3, groups, 128), i32),
            pltpu.VMEM(tap_weight.shape, f32),
            pltpu.VMEM((256, 256), bf16),
            pltpu.VMEM((2, n_theta * RT, 256), f32),
            pltpu.VMEM((n_theta * RT * 4, 128), f32),
            pltpu.VMEM((2, n_theta * RT * 4, 128), bf16),
            pltpu.VMEM((2, sources, HALF * 4, 128), bf16),
            pltpu.VMEM((sources // 4 * HALF * 4, 128), f32),
            pltpu.VMEM((2, 4, n_y, HALF, block, 128), bf16),
            pltpu.VMEM((2, 2 * QP, 4 * n_y * block), bf16),
            pltpu.VMEM((pairs, 2 * QP, 256), f32),
            pltpu.VMEM((pairs, 2, QP, 128), bf16),
            pltpu.VMEM((pairs, 2, QP, 128), bf16),
            pltpu.VMEM((2, QP, 128), bf16),
            pltpu.VMEM((2, QP, 128), bf16),
            pltpu.VMEM(((RT + 1) * QP * 4 + 8, 128), f32),
            pltpu.VMEM((2, groups, 128), i32),
            pltpu.SMEM((groups, 128), i32),
            pltpu.SMEM((groups, 128), i32),
            pltpu.SMEM((1,), i32),
            dma((slots * tiles,)), dma((tiles,)), dma((7,)), dma((2,)),
            dma((2,)), dma((2, 4)),
            dma((2, 4, 2)), dma((2, 4, 2)),
            dma((2, 4, 2)), dma((2, 4, 2)),
            dma((pairs,)), dma((pairs,)),
            dma((2,)), dma((2,)),
        ],
        compiler_params=pltpu.CompilerParams(
            collective_id=0, has_side_effects=True, vmem_limit_bytes=58 << 20
        ),
        name="convolve",
    )(wig, alm, beam, slot_order.reshape(1, -1), *cells, tap_weight, sample_count)
    return value.reshape(-1)


def solution(mesh):
    return jax.shard_map(
        shards,
        mesh=mesh,
        in_specs=(
            P(("theta", "phi"), None, None),
            P(("theta", "phi"), None, None),
            P(),
            P(),
            P(("theta", "phi")),
            P(("theta", "phi")),
            P(("theta", "phi")),
            P(None, ("theta", "phi")),
            P(("theta", "phi")),
        ),
        out_specs=P(("theta", "phi")),
        check_vma=False,
    )
```

time: 52.4 us -> 50.4 us (0.962)
  Pallas kernels: 50.2 us -> 48.2 us
  other arithmetic: 1.33 us -> 0 us
  local copies, waits for them, and re-layouts: 0 us -> 1.32 us
    pallas_call x1, Pallas kernels: 50.2 us -> 48.2 us  [shards(): pl.pallas_call(functools.partial(kernel, n_theta, n_phi, slots, ldeg, til...]
    select_n x1 -> x0, other arithmetic: 1.33 us -> none  [shards(): return jnp.where(live, value.reshape(-1), jnp.float32(0.0))]
    unnamed x0 -> x1, local copies, waits for them, and re-layouts: none -> 1.32 us
where the time goes in v4:
time: 50.4 us; the launch traced here: 50.2 us
  Pallas kernels  48.2 us (96%)
  local copies, waits for them, and re-layouts  1.32 us (3%)
  between operations  0.66 us (1%)
    pallas_call x1, Pallas kernels, shards(): pl.pallas_call(functools.partial(kernel, n_theta, n_phi, slots, ldeg, til...  48.2 us
    unnamed x1, local copies, waits for them, and re-layouts  1.32 us

profile of v4, /device:TPU:1, one launch (start us, length us, event | category | flops | bytes accessed | tf_op | source)
XLA Modules:
  0.0 50.2 jit_solution(3129731384703204805)
XLA Ops:
  0.7 48.2 %convolve.1 = f32[32,128]{1,0:T(8,128)} custom-call(bf16[4,256,8192]{2,1,0:T(8,128)(2,1)} %wig_hbm.1, bf16[4,2,8192]{2,1,0:T(2,128)(2,1)} %alm_hbm.1, bf16[8192,128]{1,0:T(8,128)(2,1)} %beam_hbm.1, s32[1,512]{1,0:T(1,128)} %bitcast.9, s32[32,128]{1,0:T(8,128)} %bitcast.6, s32[32,128]{1,0:T(8,128)} %bitcast.7, s32[32,128]{1,0:T(8,128)} %bitcast.8, ...), custom_call_target="tpu_custom_call" | custom-call | tf_op jit(solution)/shard_map/convolve/pallas_call | solution.py:496
  48.9 1.3 %copy.12 = f32[4096]{0:T(1024)} copy(f32[4096]{0:T(1024)} %bitcast.5) | data formatting | bytes 32768

commit v5 on v4

--- a/solution.py
+++ b/solution.py
@@ -13,6 +13,8 @@
 RT = 16
 QP = 208
 HALF = RT // 2
+BUNCHES = 2
+LAG = 3
 MESH = pl.DeviceIdType.MESH
 NT = (((1,), (1,)), ((), ()))
 
@@ -62,7 +64,7 @@
     total = PD * n_phi
     tiles = ldeg // tile
     sources = 2 * n_theta
-    bunch = sources // 4
+    bunch = sources // BUNCHES
     span = HALF * 4
     per_block = 4 * bunch
     wide = n_y * per_block
@@ -159,8 +161,8 @@
     q_at = q_at.astype(jnp.float32)
 
     def table(n, _):
-        sh, g = n // 4, n % 4
-        first = g * (n_theta // 4) * n_phi * slots + sh * 2
+        sh, g = n // BUNCHES, n % BUNCHES
+        first = g * (n_theta // BUNCHES) * n_phi * slots + sh * 2
         pick = (n_at == slot_col + first).astype(jnp.bfloat16)
         moved = jnp.dot(split, pick, preferred_element_type=jnp.float32)
         m_col = moved[0:1, :] * 16.0 + moved[1:2, :]
@@ -186,7 +188,7 @@
             sky_v[s, c] = jnp.broadcast_to(sky[c:c + 1, :], (16, ldeg)).astype(jnp.bfloat16)
         return 0
 
-    lax.fori_loop(0, slots, mask_sky, 0)
+    lax.fori_loop(0, 2, mask_sky, 0)
     lax.fori_loop(0, tiles, turn_beam, 0)
 
     def stage(n, _):
@@ -238,7 +240,7 @@
             def _():
                 pltpu.make_async_remote_copy(
                     src_ref=x16.at[sh, rows_of(t, c), :], dst_ref=landed.at[sh, me_t * 2 + me_c],
-                    send_sem=a_send.at[sh], recv_sem=a_recv.at[sh, me_t // (n_theta // 4)],
+                    send_sem=a_send.at[sh], recv_sem=a_recv.at[sh, me_t // (n_theta // BUNCHES)],
                     device_id=at(t, me_y, c), device_id_type=MESH,
                 ).start()
 
@@ -268,7 +270,7 @@
             device_id=at(me_t, (y_up, y_down)[h], me_c), device_id_type=MESH,
         )
 
-    own_bunch = me_t // (n_theta // 4)
+    own_bunch = me_t // (n_theta // BUNCHES)
 
     def gather(sh, g):
         @pl.when(g == own_bunch)
@@ -298,6 +300,7 @@
 
     lax.fori_loop(0, 2 * tiles, stage, 0)
     send_half(0)
+    lax.fori_loop(2, slots, mask_sky, 0)
     lax.fori_loop(2 * tiles, 4 * tiles, stage, 0)
     gather(0, 0)
     send_half(1)
@@ -319,33 +322,33 @@
         return jnp.dot(left, right, preferred_element_type=jnp.float32)
 
     def first_part(pair, _):
-        part_v[pair] = product(0, slice(0, 4), pair)
+        part_v[pair] = product(0, slice(0, BUNCHES), pair)
         return 0
 
     def second_part(pair, _):
-        part_v[pair] += product(1, slice(0, 3), pair)
+        part_v[pair] += product(1, slice(0, BUNCHES - 1), pair)
         return 0
 
     def step(n, _):
-        @pl.when(n == 4)
-        def _():
-            lax.fori_loop(0, 8, table, 0)
-
-        @pl.when(n < 8)
-        def _():
-            gather(n // 4, n % 4)
-
-        @pl.when(n >= 3)
-        def _():
-            relay((n - 3) // 4, (n - 3) % 4)
-
-        return 0
-
-    lax.fori_loop(1, 11, step, 0)
-    for g in range(4):
+        @pl.when(n == BUNCHES)
+        def _():
+            lax.fori_loop(0, 2 * BUNCHES, table, 0)
+
+        @pl.when(n < 2 * BUNCHES)
+        def _():
+            gather(n // BUNCHES, n % BUNCHES)
+
+        @pl.when(n >= LAG)
+        def _():
+            relay((n - LAG) // BUNCHES, (n - LAG) % BUNCHES)
+
+        return 0
+
+    lax.fori_loop(1, 2 * BUNCHES + LAG, step, 0)
+    for g in range(BUNCHES):
         far(0, g)
     lax.fori_loop(0, pairs, first_part, 0)
-    for g in range(3):
+    for g in range(BUNCHES - 1):
         far(1, g)
     lax.fori_loop(0, pairs, second_part, 0)
 
@@ -382,7 +385,7 @@
     def finish(n, _):
         pair = pair_at(n, me_c)
 
-        both = product(1, slice(3, 4), pair) + part_v[pair]
+        both = product(1, slice(BUNCHES - 1, BUNCHES), pair) + part_v[pair]
         for h in range(2):
             share_out[n, h] = both[QP:, h * 128:(h + 1) * 128].astype(jnp.bfloat16)
         share(n).start()
@@ -406,7 +409,7 @@
             put_cycle(me_c * HALF + 2 * pair + h, part_v[pair, :QP, h * 128:(h + 1) * 128])
         return 0
 
-    far(1, 3)
+    far(1, BUNCHES - 1)
     lax.fori_loop(0, pairs, finish, 0)
     lax.fori_loop(0, pairs, put_own, 0)
 
@@ -461,7 +464,7 @@
 
     def drain(sh, _):
         arrived(sh, 0, others).wait_send()
-        for g in range(4):
+        for g in range(BUNCHES):
             for h in range(2):
                 pass_y(sh, g, h).wait_send()
                 forward(sh, g, h).wait_send()
@@ -486,7 +489,7 @@
     tiles = ldeg // tile
     n_y = n_phi // 2
     sources = 2 * n_theta
-    block = sources
+    block = 4 * sources // BUNCHES
     pairs = HALF // 2
     groups = phi_cell.shape[0] // 128
     cells = [c.reshape(groups, 128) for c in (phi_cell, theta_cell, orient_cell_index)]
@@ -512,9 +515,9 @@
             pltpu.VMEM((n_theta * RT * 4, 128), f32),
             pltpu.VMEM((2, n_theta * RT * 4, 128), bf16),
             pltpu.VMEM((2, sources, HALF * 4, 128), bf16),
-            pltpu.VMEM((sources // 4 * HALF * 4, 128), f32),
-            pltpu.VMEM((2, 4, n_y, HALF, block, 128), bf16),
-            pltpu.VMEM((2, 2 * QP, 4 * n_y * block), bf16),
+            pltpu.VMEM((sources // BUNCHES * HALF * 4, 128), f32),
+            pltpu.VMEM((2, BUNCHES, n_y, HALF, block, 128), bf16),
+            pltpu.VMEM((2, 2 * QP, BUNCHES * n_y * block), bf16),
             pltpu.VMEM((pairs, 2 * QP, 256), f32),
             pltpu.VMEM((pairs, 2, QP, 128), bf16),
             pltpu.VMEM((pairs, 2, QP, 128), bf16),
@@ -526,9 +529,9 @@
             pltpu.SMEM((groups, 128), i32),
             pltpu.SMEM((1,), i32),
             dma((slots * tiles,)), dma((tiles,)), dma((7,)), dma((2,)),
-            dma((2,)), dma((2, 4)),
-            dma((2, 4, 2)), dma((2, 4, 2)),
-            dma((2, 4, 2)), dma((2, 4, 2)),
+            dma((2,)), dma((2, BUNCHES)),
+            dma((2, BUNCHES, 2)), dma((2, BUNCHES, 2)),
+            dma((2, BUNCHES, 2)), dma((2, BUNCHES, 2)),
             dma((pairs,)), dma((pairs,)),
             dma((2,)), dma((2,)),
         ],

time: 50.4 us -> 49.5 us (0.982)
  Pallas kernels: 48.2 us -> 47.3 us
    pallas_call x1, Pallas kernels: 48.2 us -> 47.3 us  [shards(): pl.pallas_call(functools.partial(kernel, n_theta, n_phi, slots, ldeg, til...]
where the time goes in v5:
time: 49.5 us; the launch traced here: 49.3 us
  Pallas kernels  47.3 us (96%)
  local copies, waits for them, and re-layouts  1.32 us (3%)
  between operations  0.66 us (1%)
    pallas_call x1, Pallas kernels, shards(): pl.pallas_call(functools.partial(kernel, n_theta, n_phi, slots, ldeg, til...  47.3 us
    unnamed x1, local copies, waits for them, and re-layouts  1.32 us

profile of v5, /device:TPU:1, one launch (start us, length us, event | category | flops | bytes accessed | tf_op | source)
XLA Modules:
  0.0 49.3 jit_solution(16356359480593131084)
XLA Ops:
  0.7 47.3 %convolve.1 = f32[32,128]{1,0:T(8,128)} custom-call(bf16[4,256,8192]{2,1,0:T(8,128)(2,1)} %wig_hbm.1, bf16[4,2,8192]{2,1,0:T(2,128)(2,1)} %alm_hbm.1, bf16[8192,128]{1,0:T(8,128)(2,1)} %beam_hbm.1, s32[1,512]{1,0:T(1,128)} %bitcast.9, s32[32,128]{1,0:T(8,128)} %bitcast.6, s32[32,128]{1,0:T(8,128)} %bitcast.7, s32[32,128]{1,0:T(8,128)} %bitcast.8, ...), custom_call_target="tpu_custom_call" | custom-call | tf_op jit(solution)/shard_map/convolve/pallas_call | solution.py:499
  47.9 1.3 %copy.12 = f32[4096]{0:T(1024)} copy(f32[4096]{0:T(1024)} %bitcast.5) | data formatting | bytes 32768

commit v6 on v5

--- a/solution.py
+++ b/solution.py
@@ -228,7 +228,7 @@
 
         lax.fori_loop(0, 2, to_psi, 0)
 
-        x16[sh] = x32[...].astype(jnp.bfloat16)
+        x16[sh] = x32[:n_theta * RT * 4, :].astype(jnp.bfloat16)
 
         if sh == 0:
             pl.semaphore_wait(barrier, others + 2)
@@ -281,7 +281,7 @@
         def _():
             arrived(sh, g, bunch).wait_recv()
 
-        spread[...] = landed[sh, pl.ds(g * bunch, bunch)].astype(jnp.float32).reshape(bunch * span, 128)
+        spread[:bunch * span, :] = landed[sh, pl.ds(g * bunch, bunch)].astype(jnp.float32).reshape(bunch * span, 128)
         for r in range(HALF):
             grid_v[sh, g, me_y, r] = jnp.concatenate(
                 [spread[pl.ds(r * 4 + p, bunch, stride=span), :] for p in range(4)], axis=0
@@ -512,10 +512,10 @@
             pltpu.VMEM(tap_weight.shape, f32),
             pltpu.VMEM((256, 256), bf16),
             pltpu.VMEM((2, n_theta * RT, 256), f32),
-            pltpu.VMEM((n_theta * RT * 4, 128), f32),
+            pltpu.VMEM((n_theta * RT * 4 + 8, 128), f32),
             pltpu.VMEM((2, n_theta * RT * 4, 128), bf16),
             pltpu.VMEM((2, sources, HALF * 4, 128), bf16),
-            pltpu.VMEM((sources // BUNCHES * HALF * 4, 128), f32),
+            pltpu.VMEM((sources // BUNCHES * HALF * 4 + HALF * 4, 128), f32),
             pltpu.VMEM((2, BUNCHES, n_y, HALF, block, 128), bf16),
             pltpu.VMEM((2, 2 * QP, BUNCHES * n_y * block), bf16),
             pltpu.VMEM((pairs, 2 * QP, 256), f32),

time: 49.5 us -> 49.5 us (level)
  no operation moved by 1% of the time
where the time goes in v6:
time: 49.5 us; the launch traced here: 49.3 us
  Pallas kernels  47.3 us (96%)
  local copies, waits for them, and re-layouts  1.32 us (3%)
  between operations  0.66 us (1%)
    pallas_call x1, Pallas kernels, shards(): pl.pallas_call(functools.partial(kernel, n_theta, n_phi, slots, ldeg, til...  47.3 us
    unnamed x1, local copies, waits for them, and re-layouts  1.32 us

profile of v6, /device:TPU:1, one launch (start us, length us, event | category | flops | bytes accessed | tf_op | source)
XLA Modules:
  0.0 49.3 jit_solution(12794248872288835446)
XLA Ops:
  0.7 47.3 %convolve.1 = f32[32,128]{1,0:T(8,128)} custom-call(bf16[4,256,8192]{2,1,0:T(8,128)(2,1)} %wig_hbm.1, bf16[4,2,8192]{2,1,0:T(2,128)(2,1)} %alm_hbm.1, bf16[8192,128]{1,0:T(8,128)(2,1)} %beam_hbm.1, s32[1,512]{1,0:T(1,128)} %bitcast.9, s32[32,128]{1,0:T(8,128)} %bitcast.6, s32[32,128]{1,0:T(8,128)} %bitcast.7, s32[32,128]{1,0:T(8,128)} %bitcast.8, ...), custom_call_target="tpu_custom_call" | custom-call | tf_op jit(solution)/shard_map/convolve/pallas_call | solution.py:499
  48.0 1.3 %copy.12 = f32[4096]{0:T(1024)} copy(f32[4096]{0:T(1024)} %bitcast.5) | data formatting | bytes 32768

commit v7 on v6

--- a/solution.py
+++ b/solution.py
@@ -444,7 +444,7 @@
 
     count = count_s[0]
 
-    def group(g, _):
+    def group(g):
         picked = jnp.zeros((8, 128), jnp.float32)
         for n in range(128):
             eight = taps[pl.ds(base_s[g, n], 8), :]
@@ -453,9 +453,13 @@
         weights = weight_v[:, pl.ds(pl.multiple_of(g * 128, 128), 128)]
         value = jnp.sum(picked * weights, axis=0, keepdims=True)
         out_ref[pl.ds(g, 1), :] = jnp.where(lane[0:1, :] + g * 128 < count, value, 0.0)
-        return 0
-
-    lax.fori_loop(0, groups, group, 0)
+
+    def some_groups(n, _):
+        for k in range(4):
+            group(4 * n + k)
+        return 0
+
+    lax.fori_loop(0, groups // 4, some_groups, 0)
 
     @pl.when(edge_goes)
     def _():

time: 49.5 us -> 47.5 us (0.960)
  Pallas kernels: 47.3 us -> 45.2 us
    pallas_call x1, Pallas kernels: 47.3 us -> 45.2 us  [shards(): pl.pallas_call(functools.partial(kernel, n_theta, n_phi, slots, ldeg, til...]
where the time goes in v7:
time: 47.5 us; the launch traced here: 47.2 us
  Pallas kernels  45.2 us (95%)
  local copies, waits for them, and re-layouts  1.32 us (3%)
  between operations  0.66 us (1%)
    pallas_call x1, Pallas kernels, shards(): pl.pallas_call(functools.partial(kernel, n_theta, n_phi, slots, ldeg, til...  45.2 us
    unnamed x1, local copies, waits for them, and re-layouts  1.32 us

profile of v7, /device:TPU:1, one launch (start us, length us, event | category | flops | bytes accessed | tf_op | source)
XLA Modules:
  0.0 47.2 jit_solution(518305484529337477)
XLA Ops:
  0.7 45.2 %convolve.1 = f32[32,128]{1,0:T(8,128)} custom-call(bf16[4,256,8192]{2,1,0:T(8,128)(2,1)} %wig_hbm.1, bf16[4,2,8192]{2,1,0:T(2,128)(2,1)} %alm_hbm.1, bf16[8192,128]{1,0:T(8,128)(2,1)} %beam_hbm.1, s32[1,512]{1,0:T(1,128)} %bitcast.9, s32[32,128]{1,0:T(8,128)} %bitcast.6, s32[32,128]{1,0:T(8,128)} %bitcast.7, s32[32,128]{1,0:T(8,128)} %bitcast.8, ...), custom_call_target="tpu_custom_call" | custom-call | tf_op jit(solution)/shard_map/convolve/pallas_call | solution.py:503
  45.9 1.3 %copy.12 = f32[4096]{0:T(1024)} copy(f32[4096]{0:T(1024)} %bitcast.5) | data formatting | bytes 32768
